TPU v7x, 128 devices: a whole 4x4x4 slice. The times are simulated.
128 devices in a mesh: dp: 4 (over x), expert: 32 (over z, y, core).
Axes of the slice: x: 4, y: 4, z: 4, core: 2. Of those that a mesh axis runs over, the one named last changes fastest.
Arguments:
- tokens: bfloat16 [16384, 2048], P(('dp', 'expert')), may hold values from -6 to 6
- expert_ids: int32 [16384, 8], P(('dp', 'expert')), may hold values from 0 to 63, all different within a row; in each aligned block of 128 rows (0 to 127, 128 to 255, ...) at most 18 rows name the same one
- gate_logits: float32 [16384, 8], P(('dp', 'expert')), may hold values from -400 to 400
- upstream: bfloat16 [16384, 2048], P(('dp', 'expert')), may hold values from -6 to 6
- w_gate: bfloat16 [64, 2048, 768], P('expert'), may hold values from -0.125 to 0.125
- w_up: bfloat16 [64, 2048, 768], P('expert'), may hold values from -0.125 to 0.125
- w_down: bfloat16 [64, 768, 2048], P('expert'), may hold values from -0.21875 to 0.21875
Outputs:
- grad_tokens: bfloat16 [16384, 2048], P(('dp', 'expert'))
- grad_logits: float32 [16384, 8], P(('dp', 'expert'))
- grad_gate: bfloat16 [64, 2048, 768], P('expert', 'dp')
- grad_up: bfloat16 [64, 2048, 768], P('expert', 'dp')
- grad_down: bfloat16 [64, 768, 2048], P('expert', None, 'dp')
Inputs may be any that keep to these rules, and one draw needn't show every extreme that they name: `expert_ids`: each row names 8 different experts. Among the 128 rows of one device no expert is named more than 18 times; in some device's rows one expert is named exactly 18 times.
All inputs are finite; a program needn't handle non-finite values.
Results may differ from a plain program's by a relative error of at most 0.013.
Values may be sent and summed in bfloat16 or wider, within the bound.
A program may use at most 192 MiB of HBM per device.

v0:
```python
import jax
import jax.numpy as jnp
from jax import lax
from jax.sharding import PartitionSpec as P


def expert_forward(received, w_gate, w_up):
    local_count = received.shape[0]
    width = received.shape[3]
    token_rows = received.reshape(local_count, -1, width)
    pre_gate = jnp.einsum("emd,edf->emf", token_rows, w_gate, preferred_element_type=jnp.float32)
    pre_up = jnp.einsum("emd,edf->emf", token_rows, w_up, preferred_element_type=jnp.float32)
    return (token_rows, pre_gate, pre_up)


def on_device(tokens, expert_ids, gate_logits, upstream, w_gate, w_up, w_down):
    row_count, width = tokens.shape
    top_count = expert_ids.shape[1]
    local_count = w_gate.shape[0]
    peer_count = lax.axis_size("expert")
    expert_count = local_count * peer_count
    capacity = row_count * top_count * 9 // (8 * expert_count)
    assign_count = row_count * top_count
    slot_count = local_count * peer_count * capacity
    gate_probs = jax.nn.softmax(gate_logits, axis=-1)
    gate_rounded = gate_probs.astype(jnp.bfloat16)
    flat_expert = expert_ids.reshape(-1)
    one_hot = (flat_expert[:, None] == jnp.arange(expert_count, dtype=jnp.int32)[None, :]).astype(
        jnp.int32
    )
    slot_rank = jnp.sum((jnp.cumsum(one_hot, axis=0) - one_hot) * one_hot, axis=1)
    slot_index = (
        flat_expert % local_count * peer_count + flat_expert // local_count
    ) * capacity + slot_rank
    slot_table = jnp.full((slot_count,), assign_count, jnp.int32)
    slot_table = slot_table.at[slot_index].set(jnp.arange(assign_count, dtype=jnp.int32))
    slot_token = jnp.where(slot_table < assign_count, slot_table // top_count, row_count)
    zero_row = jnp.zeros((1, width), jnp.bfloat16)
    send_shape = (local_count, peer_count, capacity, width)
    small_shape = (local_count, peer_count, capacity)
    tokens_send = jnp.concatenate([tokens, zero_row], axis=0)[slot_token].reshape(send_shape)
    upstream_send = jnp.concatenate([upstream, zero_row], axis=0)[slot_token].reshape(send_shape)
    gate_send = jnp.concatenate([gate_rounded.reshape(-1), jnp.zeros((1,), jnp.bfloat16)], axis=0)[
        slot_table
    ].reshape(small_shape)
    token_recv, upstream_recv, gate_recv = (
        lax.all_to_all(tokens_send, "expert", split_axis=1, concat_axis=1, tiled=True),
        lax.all_to_all(upstream_send, "expert", split_axis=1, concat_axis=1, tiled=True),
        lax.all_to_all(gate_send, "expert", split_axis=1, concat_axis=1, tiled=True),
    )
    token_rows, pre_gate, pre_up = expert_forward(token_recv, w_gate, w_up)
    sigmoid_gate = jax.nn.sigmoid(pre_gate)
    activated = pre_gate * sigmoid_gate
    hidden = activated * pre_up
    grad_rows = upstream_recv.reshape(local_count, -1, width)
    raw_grad = jnp.einsum("emd,efd->emf", grad_rows, w_down, preferred_element_type=jnp.float32)
    slot_dgate = jnp.sum(raw_grad * hidden, axis=-1).astype(jnp.bfloat16)
    gate_column = gate_recv.reshape(local_count, -1, 1).astype(jnp.float32)
    d_hidden = gate_column * raw_grad
    weighted_hidden = (gate_column * hidden).astype(jnp.bfloat16)
    down_part = jnp.einsum(
        "emf,emd->efd", weighted_hidden, grad_rows, preferred_element_type=jnp.float32
    )
    d_pre_gate = (
        d_hidden * pre_up * sigmoid_gate * (1.0 + pre_gate * (1.0 - sigmoid_gate))
    ).astype(jnp.bfloat16)
    d_pre_up = (d_hidden * activated).astype(jnp.bfloat16)
    slot_dx = (
        jnp.einsum("emf,edf->emd", d_pre_gate, w_gate, preferred_element_type=jnp.float32)
        + jnp.einsum("emf,edf->emd", d_pre_up, w_up, preferred_element_type=jnp.float32)
    ).astype(jnp.bfloat16)
    back_dx, back_dgate = (
        lax.all_to_all(
            slot_dx.reshape(send_shape), "expert", split_axis=1, concat_axis=1, tiled=True
        ),
        lax.all_to_all(
            slot_dgate.reshape(small_shape), "expert", split_axis=1, concat_axis=1, tiled=True
        ),
    )
    gate_part = jnp.einsum(
        "emd,emf->edf", token_rows, d_pre_gate, preferred_element_type=jnp.float32
    )
    up_part = jnp.einsum("emd,emf->edf", token_rows, d_pre_up, preferred_element_type=jnp.float32)
    gate_share, up_share, down_share = (
        lax.psum_scatter(
            gate_part.astype(jnp.bfloat16), "dp", scatter_dimension=1, tiled=True
        ).astype(jnp.float32),
        lax.psum_scatter(
            up_part.astype(jnp.bfloat16), "dp", scatter_dimension=1, tiled=True
        ).astype(jnp.float32),
        lax.psum_scatter(
            down_part.astype(jnp.bfloat16), "dp", scatter_dimension=2, tiled=True
        ).astype(jnp.float32),
    )
    gathered_dx = back_dx.reshape(slot_count, width)[slot_index].reshape(
        row_count, top_count, width
    )
    grad_tokens = jnp.sum(gathered_dx.astype(jnp.float32), axis=1).astype(jnp.bfloat16)
    dgate_rows = (
        back_dgate.reshape(slot_count)[slot_index].astype(jnp.float32).reshape(row_count, top_count)
    )
    grad_logits = gate_probs * (
        dgate_rows - jnp.sum(gate_probs * dgate_rows, axis=-1, keepdims=True)
    )
    return (
        grad_tokens,
        grad_logits,
        gate_share.astype(jnp.bfloat16),
        up_share.astype(jnp.bfloat16),
        down_share.astype(jnp.bfloat16),
    )


def solution(mesh):
    in_specs = (
        P(("dp", "expert"), None),
        P(("dp", "expert"), None),
        P(("dp", "expert"), None),
        P(("dp", "expert"), None),
        P("expert", None, None),
        P("expert", None, None),
        P("expert", None, None),
    )
    out_specs = (
        P(("dp", "expert"), None),
        P(("dp", "expert"), None),
        P("expert", "dp", None),
        P("expert", "dp", None),
        P("expert", None, "dp"),
    )
    return jax.shard_map(
        on_device, mesh=mesh, in_specs=in_specs, out_specs=out_specs, check_vma=False
    )
```

profile of v0, /device:TPU:1, one launch (start us, length us, event | category | flops | bytes accessed | tf_op | source)
XLA Modules:
  0.0 421.6 jit_solution(16998598510501320982)
XLA Ops:
  7.2 0.8 copy.55
  8.0 0.1 eq.31
  8.1 0.1 eq.27
  8.2 0.1 reshape.201
  8.3 0.7 reduce_max.9
  9.0 0.7 fusion.24
  9.7 0.7 fusion.25
  10.4 0.1 copy.54
  10.5 0.1 reshape.200
  10.7 18.0 %reduce-window.6 = s32[64,8,128]{2,1,0:T(8,128)S(1)} reduce-window(s32[64,8,128]{2,1,0:T(8,128)S(1)} %fusion.15, s32[]{:T(128)} %constant.58.clone.1), window={size=1x1x128 pad=0_0x0_0x127_0}, to_apply=%region_2.0 | reduce-window | flops 8323072 | bytes 524292 | tf_op jit(solution)/shard_map/reduce-window
  28.7 0.1 slice.18
  28.8 0.1 copy.58
  29.0 0.1 copy.59
  29.1 0.1 broadcast_add_fusion
  29.2 0.1 fusion.14
  29.4 4.3 %scatter_custom_fusion = s32[1152]{0:T(1024)S(1)} fusion(s32[1024]{0:T(1024)S(1)} %bitcast.39, s32[1024]{0:T(1024)S(1)} %iota.11, s32[]{:T(128)} %constant.57.clone.1), kind=kCustom, calls=%fused_computation.59 | custom fusion | bytes 4612 | tf_op jit(solution)/shard_map/scatter | solution.py:36
  33.7 7.3 %gather_fusion = bf16[1152]{0:T(1024)(128)(2,1)S(1)} fusion(bf16[1025]{0:T(1024)(128)(2,1)S(1)} %pad_maximum_fusion, s32[2048]{0:T(1024)S(1)} %get-tuple-element.21), kind=kCustom, calls=%fused_computation | custom fusion | bytes 9216 | tf_op jit(solution)/shard_map/gather | solution.py:43
  41.0 0.1 reshape.203
  41.2 0.6 copy.60
  41.8 9.6 %all-to-all-start = ((bf16[2,32,18]{2,0,1:T(2,128)(2,1)}), bf16[2,32,18]{2,0,1:T(2,128)(2,1)S(1)}, u32[]{:S(2)}, u32[]{:S(2)}) async-start(bf16[2,32,18]{2,0,1:T(2,128)(2,1)} %copy.60), calls=%async_computation | async-start | bytes 32768 | tf_op jit(solution)/shard_map/all_to_all | solution.py:49
  51.5 6.1 %gather_fusion.2 = bf16[1152,2048]{1,0:T(8,128)(2,1)} fusion(bf16[129,2048]{1,0:T(8,128)(2,1)S(1)} %concatenate.11, s32[2048]{0:T(1024)S(1)} %get-tuple-element.20), kind=kCustom, calls=%fused_computation.2 | custom fusion | bytes 9441792 | tf_op jit(solution)/shard_map/gather | solution.py:41
  57.5 7.6 %reshape.206 = bf16[2,32,18,2048]{3,2,1,0:T(8,128)(2,1)} reshape(bf16[1152,2048]{1,0:T(8,128)(2,1)} %gather_fusion.2) | data formatting | bytes 9437184 | tf_op jit(solution)/shard_map/reshape | solution.py:41
  65.1 9.9 %copy.65 = bf16[2,32,18,2048]{3,0,2,1:T(2,128)(2,1)} copy(bf16[2,32,18,2048]{3,2,1,0:T(8,128)(2,1)} %reshape.206) | data formatting | bytes 9437184 | tf_op jit(solution)/shard_map/reshape | solution.py:41
  75.0 0.0 all-to-all-done
  75.0 8.0 %all-to-all-start.2 = ((bf16[2,32,18,2048]{3,0,2,1:T(2,128)(2,1)}), bf16[2,32,18,2048]{3,0,2,1:T(2,128)(2,1)}, u32[]{:S(2)}, u32[]{:S(2)}) async-start(bf16[2,32,18,2048]{3,0,2,1:T(2,128)(2,1)} %copy.65), calls=%async_computation.2 | async-start | bytes 9437184 | tf_op jit(solution)/shard_map/all_to_all | solution.py:47
  83.0 6.0 %gather_fusion.1 = bf16[1152,2048]{1,0:T(8,128)(2,1)} fusion(bf16[129,2048]{1,0:T(8,128)(2,1)S(1)} %concatenate.10, s32[2048]{0:T(1024)S(1)} %get-tuple-element.20), kind=kCustom, calls=%fused_computation.1 | custom fusion | bytes 9441792 | tf_op jit(solution)/shard_map/gather | solution.py:42
  89.0 7.6 %reshape.204 = bf16[2,32,18,2048]{3,2,1,0:T(8,128)(2,1)} reshape(bf16[1152,2048]{1,0:T(8,128)(2,1)} %gather_fusion.1) | data formatting | bytes 9437184 | tf_op jit(solution)/shard_map/reshape | solution.py:42
  96.6 9.9 %copy.63 = bf16[2,32,18,2048]{3,0,2,1:T(2,128)(2,1)} copy(bf16[2,32,18,2048]{3,2,1,0:T(8,128)(2,1)} %reshape.204) | data formatting | bytes 9437184 | tf_op jit(solution)/shard_map/reshape | solution.py:42
  106.5 32.1 %all-to-all-done.2 = bf16[2,32,18,2048]{3,0,2,1:T(2,128)(2,1)} async-done(((bf16[2,32,18,2048]{3,0,2,1:T(2,128)(2,1)}), bf16[2,32,18,2048]{3,0,2,1:T(2,128)(2,1)}, u32[]{:S(2)}, u32[]{:S(2)}) %all-to-all-start.2) | async-done | bytes 4718624 | tf_op jit(solution)/shard_map/all_to_all | solution.py:47
  138.6 8.7 %all-to-all-start.1 = ((bf16[2,32,18,2048]{3,0,2,1:T(2,128)(2,1)}), bf16[2,32,18,2048]{3,0,2,1:T(2,128)(2,1)}, u32[]{:S(2)}, u32[]{:S(2)}) async-start(bf16[2,32,18,2048]{3,0,2,1:T(2,128)(2,1)} %copy.63), calls=%async_computation.1 | async-start | bytes 9437184 | tf_op jit(solution)/shard_map/all_to_all | solution.py:48
  147.3 0.3 reduce-scatter.8.cloned.1.call-start
  147.6 0.1 copy.61
  147.7 0.1 copy.62
  147.8 0.1 reshape.212
  147.9 10.5 %fusion.6 = f32[2,576,768]{2,1,0:T(8,128)} fusion(bf16[2,2048,768]{2,1,0:T(8,128)(2,1)} %param.11, bf16[2,576,2048]{2,0,1:T(2,128)(2,1)} %bitcast.5), kind=kOutput, calls=%fused_computation.22 | convolution fusion | flops 3623878656 | bytes 14548992 | tf_op jit(solution)/shard_map/emd,edf->emf/dot_general | solution.py:11
  158.4 10.5 %fusion.8 = f32[2,576,768]{2,1,0:T(8,128)} fusion(bf16[2,2048,768]{2,1,0:T(8,128)(2,1)} %param.12, bf16[2,576,2048]{2,0,1:T(2,128)(2,1)} %bitcast.5), kind=kOutput, calls=%fused_computation.24 | convolution fusion | flops 3623878656 | bytes 14548992 | tf_op jit(solution)/shard_map/emd,edf->emf/dot_general | solution.py:12
  168.9 34.2 %all-to-all-done.1 = bf16[2,32,18,2048]{3,0,2,1:T(2,128)(2,1)} async-done(((bf16[2,32,18,2048]{3,0,2,1:T(2,128)(2,1)}), bf16[2,32,18,2048]{3,0,2,1:T(2,128)(2,1)}, u32[]{:S(2)}, u32[]{:S(2)}) %all-to-all-start.1) | async-done | bytes 4718624 | tf_op jit(solution)/shard_map/all_to_all | solution.py:48
  203.1 13.9 %convolution_convert_fusion = bf16[2,768,2048]{2,1,0:T(8,128)(2,1)} fusion(bf16[2,576,2048]{2,0,1:T(2,128)(2,1)} %bitcast.4, f32[2,576]{1,0:T(2,128)S(1)} %reshape.212, f32[2,576,768]{2,1,0:T(8,128)} %fusion.8, f32[2,576,768]{2,1,0:T(8,128)} %fusion.6), kind=kOutput, calls=%fused_computation.7 | convolution fusion | flops 3633217536 | bytes 18092544 | tf_op jit(solution)/shard_map/emf,emd->efd/dot_general | solution.py:61
  217.0 0.0 reduce-scatter.8.cloned.1.call-update
  217.0 0.0 reduce-scatter.4.cloned.1.call-start
  217.1 12.7 %multiply_reduce_fusion = (bf16[2,576]{1,0:T(2,128)(2,1)S(1)}, bf16[2,576,768]{2,1,0:T(8,128)(2,1)S(1)}, bf16[2,576,768]{2,1,0:T(8,128)(2,1)S(1)}) fusion(f32[2,576,768]{2,1,0:T(8,128)} %fusion.8, f32[2,576,768]{2,1,0:T(8,128)} %fusion.6, f32[2,576]{1,0:T(2,128)S(1)} %reshape.212, bf16[2,768,2048]{2,1,0:T(8,128)(2,1)} %param.13, ...), kind=kOutput, calls=%fused_computation.15 | convolution fusion | flops 3638918144 | bytes 21633792 | tf_op jit(solution)/shard_map/emd,efd->emf/dot_general | solution.py:56
  229.8 1.2 copy-done.3
  231.0 19.0 %convolution_convert_fusion.2 = bf16[2,2048,768]{2,1,0:T(8,128)(2,1)} fusion(bf16[2,576,768]{2,1,0:T(8,128)(2,1)S(1)} %get-tuple-element.16, bf16[2,576,2048]{2,0,1:T(2,128)(2,1)} %bitcast.5), kind=kOutput, calls=%fused_computation.9 | convolution fusion | flops 3627024384 | bytes 12779520 | tf_op jit(solution)/shard_map/emd,emf->edf/dot_general | solution.py:80
  250.0 0.0 reduce-scatter.4.cloned.1.call-update
  250.0 0.0 reduce-scatter.6.cloned.1.call-start
  250.0 18.9 %convolution_convert_fusion.1 = bf16[2,2048,768]{2,1,0:T(8,128)(2,1)} fusion(bf16[2,576,768]{2,1,0:T(8,128)(2,1)S(1)} %get-tuple-element.17, bf16[2,576,2048]{2,0,1:T(2,128)(2,1)} %bitcast.5), kind=kOutput, calls=%fused_computation.8 | convolution fusion | flops 3627024384 | bytes 12779520 | tf_op jit(solution)/shard_map/emd,emf->edf/dot_general | solution.py:83
  269.0 0.0 reduce-scatter.6.cloned.1.call-update
  269.0 0.1 convert_element_type.73
  269.1 0.6 copy.70
  269.8 9.0 %all-to-all-start.4 = ((bf16[2,32,18]{2,0,1:T(2,128)(2,1)}), bf16[2,32,18]{2,0,1:T(2,128)(2,1)S(1)}, u32[]{:S(2)}, u32[]{:S(2)}) async-start(bf16[2,32,18]{2,0,1:T(2,128)(2,1)} %copy.70), calls=%async_computation.4 | async-start | bytes 32768 | tf_op jit(solution)/shard_map/all_to_all | solution.py:76
  278.7 11.0 %fusion.27 = f32[2,576,2048]{2,1,0:T(8,128)} fusion(bf16[2,576,768]{2,1,0:T(8,128)(2,1)} %copy-done.3, bf16[2,2048,768]{2,1,0:T(8,128)(2,1)} %param.11), kind=kOutput, calls=%fused_computation.66 | convolution fusion | flops 3623878656 | bytes 17498112 | tf_op jit(solution)/shard_map/emf,edf->emd/dot_general | solution.py:69
  289.7 10.9 %add_convert_fusion = bf16[2,576,2048]{2,1,0:T(8,128)(2,1)} fusion(f32[2,576,2048]{2,1,0:T(8,128)} %fusion.27, bf16[2,576,768]{2,1,0:T(8,128)(2,1)S(1)} %get-tuple-element.17, bf16[2,2048,768]{2,1,0:T(8,128)(2,1)} %param.12), kind=kOutput, calls=%fused_computation.6 | convolution fusion | flops 3628597248 | bytes 22216704 | tf_op jit(solution)/shard_map/emf,edf->emd/dot_general | solution.py:70
  300.5 9.4 %copy.68 = bf16[2,576,2048]{2,0,1:T(2,128)(2,1)} copy(bf16[2,576,2048]{2,1,0:T(8,128)(2,1)} %add_convert_fusion) | data formatting | bytes 9437184 | tf_op jit(solution)/shard_map/convert_element_type | solution.py:71
  310.0 8.0 %all-to-all-start.3 = ((bf16[2,32,18,2048]{3,0,2,1:T(2,128)(2,1)}), bf16[2,32,18,2048]{3,0,2,1:T(2,128)(2,1)}, u32[]{:S(2)}, u32[]{:S(2)}) async-start(bf16[2,32,18,2048]{3,0,2,1:T(2,128)(2,1)} %bitcast.35), calls=%async_computation.3 | async-start | bytes 9437184 | tf_op jit(solution)/shard_map/all_to_all | solution.py:73
  318.0 0.1 reshape.211
  318.1 6.8 %gather_fusion.4 = bf16[1024]{0:T(1024)(128)(2,1)S(1)} fusion(bf16[1152]{0:T(1024)(128)(2,1)S(1)} %reshape.211, s32[1024]{0:T(1024)S(1)} %broadcast_clamp_fusion), kind=kCustom, calls=%fused_computation.4 | custom fusion | bytes 8192 | tf_op jit(solution)/shard_map/gather | solution.py:100
  325.0 0.1 reshape.213
  325.1 0.6 subtract_multiply_fusion
  325.8 47.8 %all-to-all-done.3 = bf16[2,32,18,2048]{3,0,2,1:T(2,128)(2,1)} async-done(((bf16[2,32,18,2048]{3,0,2,1:T(2,128)(2,1)}), bf16[2,32,18,2048]{3,0,2,1:T(2,128)(2,1)}, u32[]{:S(2)}, u32[]{:S(2)}) %all-to-all-start.3) | async-done | bytes 4718624 | tf_op jit(solution)/shard_map/all_to_all | solution.py:73
  373.6 7.5 %copy.69 = bf16[2,32,18,2048]{3,2,1,0:T(8,128)(2,1)} copy(bf16[2,32,18,2048]{3,0,2,1:T(2,128)(2,1)} %all-to-all-done.3) | data formatting | bytes 9437184 | tf_op jit(solution)/shard_map/all_to_all | solution.py:73
  381.0 7.8 %reshape.209 = bf16[1152,2048]{1,0:T(8,128)(2,1)} reshape(bf16[2,32,18,2048]{3,2,1,0:T(8,128)(2,1)} %copy.69) | data formatting | bytes 9437184 | tf_op jit(solution)/shard_map/reshape | solution.py:95
  388.9 11.8 %gather_fusion.3 = bf16[1024,2048]{1,0:T(8,128)(2,1)} fusion(bf16[1152,2048]{1,0:T(8,128)(2,1)} %reshape.209, s32[1024]{0:T(1024)S(1)} %broadcast_clamp_fusion), kind=kCustom, calls=%fused_computation.3 | custom fusion | bytes 8392704 | tf_op jit(solution)/shard_map/gather | solution.py:95
  400.7 6.0 %bitcast_reduce_fusion = bf16[128,2048]{1,0:T(8,128)(2,1)} fusion(bf16[1024,2048]{1,0:T(8,128)(2,1)} %gather_fusion.3), kind=kLoop, calls=%fused_computation.10 | loop fusion | flops 1835008 | bytes 4718592 | tf_op jit(solution)/shard_map/reduce_sum | solution.py:98
  406.7 7.9 %reduce-scatter.6.cloned.1.call-done = bf16[2,512,768]{2,1,0:T(8,128)(2,1)} async-done(((bf16[2,2048,768]{2,1,0:T(8,128)(2,1)}), bf16[2,512,768]{2,1,0:T(8,128)(2,1)}) %reduce-scatter.6.cloned.1.call-update) | async-done | bytes 1572880 | tf_op jit(solution)/shard_map/reduce_scatter | solution.py:88
  (24 shorter events, 0.3 us)
Async XLA Ops:
  7.2 44.2 %copy-start = (bf16[128,2048]{1,0:T(8,128)(2,1)S(1)}, bf16[128,2048]{1,0:T(8,128)(2,1)}, u32[]{:S(2)}) copy-start(bf16[128,2048]{1,0:T(8,128)(2,1)} %param.7) | copy-start | bytes 1572868
  41.8 33.2 %all-to-all-start = ((bf16[2,32,18]{2,0,1:T(2,128)(2,1)}), bf16[2,32,18]{2,0,1:T(2,128)(2,1)S(1)}, u32[]{:S(2)}, u32[]{:S(2)}) async-start(bf16[2,32,18]{2,0,1:T(2,128)(2,1)} %copy.60), calls=%async_computation | async-start | bytes 32768 | tf_op jit(solution)/shard_map/all_to_all | solution.py:49
  75.0 8.0 %copy-start.1 = (bf16[128,2048]{1,0:T(8,128)(2,1)S(1)}, bf16[128,2048]{1,0:T(8,128)(2,1)}, u32[]{:S(2)}) copy-start(bf16[128,2048]{1,0:T(8,128)(2,1)} %param.10) | copy-start | bytes 1572868
  75.0 63.5 %all-to-all-start.2 = ((bf16[2,32,18,2048]{3,0,2,1:T(2,128)(2,1)}), bf16[2,32,18,2048]{3,0,2,1:T(2,128)(2,1)}, u32[]{:S(2)}, u32[]{:S(2)}) async-start(bf16[2,32,18,2048]{3,0,2,1:T(2,128)(2,1)} %copy.65), calls=%async_computation.2 | async-start | bytes 9437184 | tf_op jit(solution)/shard_map/all_to_all | solution.py:47
  138.6 64.5 %all-to-all-start.1 = ((bf16[2,32,18,2048]{3,0,2,1:T(2,128)(2,1)}), bf16[2,32,18,2048]{3,0,2,1:T(2,128)(2,1)}, u32[]{:S(2)}, u32[]{:S(2)}) async-start(bf16[2,32,18,2048]{3,0,2,1:T(2,128)(2,1)} %copy.63), calls=%async_computation.1 | async-start | bytes 9437184 | tf_op jit(solution)/shard_map/all_to_all | solution.py:48
  147.3 259.5 %reduce-scatter.8.cloned.1.call-start = ((), (), s32[]{:S(2)}) async-start(), calls=%async_computation.10 | async-start | bytes 7864320 | tf_op jit(solution)/shard_map/reduce_scatter | solution.py:91
  217.0 189.7 %reduce-scatter.4.cloned.1.call-start = ((), (), s32[]{:S(2)}) async-start(), calls=%async_computation.8 | async-start | bytes 7864320 | tf_op jit(solution)/shard_map/reduce_scatter | solution.py:85
  229.8 1.2 copy-start.3
  250.0 164.6 %reduce-scatter.6.cloned.1.call-start = ((), (), s32[]{:S(2)}) async-start(), calls=%async_computation.9 | async-start | bytes 7864320 | tf_op jit(solution)/shard_map/reduce_scatter | solution.py:88
  269.8 40.2 %all-to-all-start.4 = ((bf16[2,32,18]{2,0,1:T(2,128)(2,1)}), bf16[2,32,18]{2,0,1:T(2,128)(2,1)S(1)}, u32[]{:S(2)}, u32[]{:S(2)}) async-start(bf16[2,32,18]{2,0,1:T(2,128)(2,1)} %copy.70), calls=%async_computation.4 | async-start | bytes 32768 | tf_op jit(solution)/shard_map/all_to_all | solution.py:76
  310.0 15.1 %copy-start.2 = (f32[128,8]{0,1:T(8,128)S(1)}, f32[128,8]{0,1:T(8,128)}, u32[]{:S(2)}) copy-start(f32[128,8]{0,1:T(8,128)} %param.9) | copy-start | bytes 12292
  310.0 63.6 %all-to-all-start.3 = ((bf16[2,32,18,2048]{3,0,2,1:T(2,128)(2,1)}), bf16[2,32,18,2048]{3,0,2,1:T(2,128)(2,1)}, u32[]{:S(2)}, u32[]{:S(2)}) async-start(bf16[2,32,18,2048]{3,0,2,1:T(2,128)(2,1)} %bitcast.35), calls=%async_computation.3 | async-start | bytes 9437184 | tf_op jit(solution)/shard_map/all_to_all | solution.py:73
Sparse Core Ops, SparseCore 0:
  217.2 64.0 reduce-scatter.7
  284.3 63.6 reduce-scatter.3
  350.9 63.6 reduce-scatter.5
where the time goes:
time: 430 us; the launch traced here: 422 us
  waiting for transfers between devices  122 us (28%)
  local copies, waits for them, and re-layouts  107 us (25%)
  matrix products  107 us (25%)
  starting transfers between devices  43.6 us (10%)
  other arithmetic  27.1 us (6%)
  between operations  14.4 us (3%)
    all_to_all x1, waiting for transfers between devices, on_device(): lax.all_to_all(slot_dx.reshape(send_shape), 'expert', split_axis=1, conca...  47.8 us
    all_to_all x1, waiting for transfers between devices, on_device(): lax.all_to_all(upstream_send, 'expert', split_axis=1, concat_axis=1, tile...  34.2 us
    all_to_all x1, waiting for transfers between devices, on_device(): lax.all_to_all(tokens_send, 'expert', split_axis=1, concat_axis=1, tiled=...  32.1 us
    dot_general x1, matrix products, on_device(): jnp.einsum('emd,emf->edf', token_rows, d_pre_gate, preferred_element_type...  19 us
    dot_general x1, matrix products, on_device(): jnp.einsum('emd,emf->edf', token_rows, d_pre_up, preferred_element_type=j...  18.9 us
    another operation x3, other arithmetic  18.2 us
    reshape x2, local copies, waits for them, and re-layouts, on_device(): jnp.concatenate([tokens, zero_row], axis=0)[slot_token].reshape(send_shape)  17.5 us
    reshape x2, local copies, waits for them, and re-layouts, on_device(): jnp.concatenate([upstream, zero_row], axis=0)[slot_token]  17.5 us
  transfers between devices with their start and end apart: 8, of which 4 were waited for; matrix products, arithmetic and copies ran while one was open for 46% of the time, Pallas kernels for 0%

commit v1 on v0

v1 whole, which is shorter than its diff:
```python
import jax
import jax.numpy as jnp
from jax import lax
from jax.experimental import pallas as pl
from jax.experimental.pallas import tpu as pltpu
from jax.sharding import PartitionSpec as P

MESH = pl.DeviceIdType.MESH
BF = jnp.bfloat16
F32 = jnp.float32
D, FF, NE, NX = 2048, 768, 32, 4
MAIN, OVF = 16, 2
ROWS = NE * (MAIN + OVF)
BACK = D + 256 + 128
ANY = pl.BlockSpec(memory_space=pl.ANY)
VMEM = pl.BlockSpec(memory_space=pltpu.VMEM)


def iota(shape, dim):
    return lax.broadcasted_iota(jnp.int32, shape, dim)


def dot_nt(a, b):
    return lax.dot_general(a, b, (((1,), (1,)), ((), ())), preferred_element_type=F32)


def dot_tn(a, b):
    return lax.dot_general(a, b, (((0,), (0,)), ((), ())), preferred_element_type=F32)


def dot(a, b):
    return jnp.dot(a, b, preferred_element_type=F32)


def routing_table(ids, gate_rounded):
    expert = iota((128, 64), 1)
    routed = jnp.zeros((128, 64), F32)
    gates = jnp.zeros((128, 64), F32)
    for k in range(8):
        hit = ids[:, k : k + 1] == expert
        routed = routed + jnp.where(hit, 1.0, 0.0)
        gates = gates + jnp.where(hit, gate_rounded[:, k : k + 1], 0.0)
    before = jnp.where(iota((128, 128), 1) < iota((128, 128), 0), 1.0, 0.0)
    rank = dot(before.astype(BF), routed.astype(BF))
    return jnp.concatenate([jnp.where(routed > 0, rank + 1.0, 0.0), gates], axis=1).astype(BF)


def slot_targets():
    row, lane = iota((80, 256), 0), iota((80, 256), 1)
    over = row - 64
    core = jnp.where(row < 64, (row % 32) // 16, (over % 4) // 2)
    slot = jnp.where(row < 64, row % 16, 16 + over % 2)
    ok = (core == lane // 128) & (row < 72)
    second = ((row >= 32) & (row < 64)) | (over >= 4)
    return jnp.where(ok, slot + 1, -1).astype(F32), jnp.where(second, 1.0, 0.0)


def kernel(
    tg, ug, wg, wu, wd, tab, ids, probs,
    gtok, glog, gg, gu, gd, rb, back,
    stage, pmat, xs, us, ov, xgate, wgv, wuv, wdv, pre_g, pre_u, wh, dgu, dgacc,
    sa, ra, sb, rbv, own, outv, outd, dxs, bkv, tokacc,
    stage_sem, w_sem, sa_s, ra_r, sb_s, rb_r, bk_s, bk_r, ld_sem, out_sem,
):
    x, me = lax.axis_index("dp"), lax.axis_index("expert")
    right, left = lax.rem(x + 1, NX), lax.rem(x + 3, NX)

    barrier = pltpu.get_barrier_semaphore()

    def greet(i, c):
        pl.semaphore_signal(barrier, inc=1, device_id=(x, lax.rem(me + i, NE)), device_id_type=MESH)
        return c

    lax.fori_loop(1, NE, greet, 0)
    for other in (right, left):
        pl.semaphore_signal(barrier, inc=1, device_id=(other, me), device_id_type=MESH)

    def wload(e):
        return [
            pltpu.make_async_copy(wg.at[e], wgv, w_sem.at[0]),
            pltpu.make_async_copy(wu.at[e], wuv, w_sem.at[1]),
        ]

    def wdload(e):
        return pltpu.make_async_copy(wd.at[e], wdv, w_sem.at[2])

    def start_weights(e):
        for cp in wload(e):
            cp.start()

    start_weights(0)
    wdload(0).start()

    target, second = slot_targets()

    def dispatch(src, dst, table):
        w = src.shape[2]

        def load(j, slot):
            return pltpu.make_async_copy(src.at[j], stage.at[slot, :, pl.ds(0, w)], stage_sem.at[slot])

        load(0, 0).start()

        def body(j, c):
            slot = lax.rem(j, 2)

            @pl.when(j + 1 < 16)
            def _():
                load(j + 1, 1 - slot).start()

            load(j, slot).wait()
            if table:
                tabj = stage[slot, :, D : D + 128]
                pick = jnp.where(iota((8, 128), 1) == 2 * me + iota((8, 128), 0), 1.0, 0.0).astype(BF)
                ranks = dot_nt(pick, tabj)
                row0 = jnp.broadcast_to(ranks[0:1, :], (80, 256))
                row1 = jnp.broadcast_to(ranks[1:2, :], (80, 256))
                pm = jnp.where(jnp.where(second > 0.5, row1, row0) == target, 1.0, 0.0).astype(BF)
                pmat[j] = pm
                got = dot(pm, tabj)
                at = pl.multiple_of(32 * j, 32)
                xgate[0, pl.ds(at, 32), :] = got[0:32]
                xgate[1, pl.ds(at, 32), :] = got[32:64]
                ov[pl.ds(pl.multiple_of(8 * j, 8), 8), D : D + 128] = got[64:72]
            pm = pmat[j]
            for n in range(D // 512):
                cols = slice(512 * n, 512 * n + 512)
                got = dot(pm, stage[slot, :, cols])
                at = pl.multiple_of(32 * j, 32)
                dst[0, pl.ds(at, 32), cols] = got[0:32].astype(BF)
                dst[1, pl.ds(at, 32), cols] = got[32:64].astype(BF)
                ov[pl.ds(pl.multiple_of(8 * j, 8), 8), cols] = got[64:72]
            return c

        lax.fori_loop(0, 16, body, 0)
        r, col = iota((64, 128), 0), iota((64, 128), 1)
        for e in range(2):
            sel = jnp.where(col == 8 * (r // 4) + 4 * e + r % 4, 1.0, 0.0).astype(BF)
            for n in range(D // 512):
                cols = slice(512 * n, 512 * n + 512)
                dst[e, 512:576, cols] = dot(sel, ov[:, cols].astype(BF)).astype(BF)
            if table:
                xgate[e, 512:576, :] = dot(sel, ov[:, D : D + 128].astype(BF))

    dispatch(tg, xs, True)
    pl.semaphore_wait(barrier, NE - 1 + 2)

    def gate_of(e, rows):
        lane = iota((rows.size, 128), 1)
        return jnp.sum(jnp.where(lane == 64 + 2 * me + e, xgate[e, rows, :], 0.0), axis=1, keepdims=True)

    def forward(e):
        for cp in wload(e):
            cp.wait()

        def body(i, c):
            rows = pl.ds(pl.multiple_of((i // 3) * 192, 192), 192)
            cols = pl.ds(pl.multiple_of((i % 3) * 256, 256), 256)
            pg = dot(xs[e, rows, :], wgv[:, cols])
            pu = dot(xs[e, rows, :], wuv[:, cols])
            pre_g[e, rows, cols] = pg
            pre_u[e, rows, cols] = pu
            hidden = pg * jax.nn.sigmoid(pg) * pu
            wh[e, rows, cols] = (gate_of(e, rows) * hidden).astype(BF)
            return c

        lax.fori_loop(0, 9, body, 0)

    def backward(e):
        wdload(e).wait()

        def body(i, c):
            rows = pl.ds(pl.multiple_of((i // 3) * 192, 192), 192)
            cols = pl.ds(pl.multiple_of((i % 3) * 256, 256), 256)
            raw = dot_nt(us[e, rows, :], wdv[cols, :])
            pg, pu = pre_g[e, rows, cols], pre_u[e, rows, cols]
            s = jax.nn.sigmoid(pg)
            act = pg * s
            part = raw * (act * pu)
            part = part[:, 0:128] + part[:, 128:256]
            dgacc[e, rows, :] = jnp.where(i % 3 == 0, jnp.zeros_like(part), dgacc[e, rows, :]) + part
            dh = gate_of(e, rows) * raw
            dgu[e, 0, rows, cols] = (dh * pu * s * (1.0 + pg * (1.0 - s))).astype(BF)
            dgu[e, 1, rows, cols] = (dh * act).astype(BF)
            return c

        lax.fori_loop(0, 9, body, 0)
        if e == 0:
            wdload(1).start()

    def input_grad(e):
        for cp in wload(e):
            cp.wait()

        def body(i, c):
            rows = pl.ds(pl.multiple_of((i // 4) * 192, 192), 192)
            cols = pl.ds(pl.multiple_of((i % 4) * 512, 512), 512)
            dx = dot_nt(dgu[e, 0, rows, :], wgv[cols, :]) + dot_nt(dgu[e, 1, rows, :], wuv[cols, :])
            dxs[e, rows, cols] = dx.astype(BF)
            return c

        lax.fori_loop(0, 12, body, 0)
        r, col = iota((512, 64), 0), iota((512, 64), 1)
        place = 2 * (r // 16) + (r % 16) // 8 == col
        packed = jnp.zeros((512, 256), F32)
        for q in range(8):
            sel = jnp.where(place & (r % 8 == q), 1.0, 0.0).astype(BF)
            packed = packed + dot(sel, dxs[e, 512:576, 256 * q : 256 * q + 256])
        dxs[e, 0:512, D : D + 256] = packed.astype(BF)
        dgate = jnp.sum(dgacc[e], axis=1, keepdims=True).astype(BF).astype(F32)
        first = iota((512, 128), 1) == 0
        sel = jnp.where(place & (r % 8 == 0), 1.0, 0.0).astype(BF)
        over = dot(sel, jnp.broadcast_to(dgate[512:576], (64, 128)).astype(BF))
        main = jnp.broadcast_to(dgate[0:512], (512, 128))
        dxs[e, 0:512, D + 256 :] = jnp.where(first, main, over).astype(BF)

    def send_back(e):
        pltpu.make_async_copy(dxs.at[e, pl.ds(pl.multiple_of(16 * me, 16), 16)], back.at[e, me], ld_sem.at[2]).start()

        def body(i, c):
            p = lax.rem(me + i, NE)
            pltpu.make_async_remote_copy(
                src_ref=dxs.at[e, pl.ds(pl.multiple_of(16 * p, 16), 16)],
                dst_ref=back.at[e, me],
                send_sem=bk_s.at[e],
                recv_sem=bk_r.at[e],
                device_id=(x, p),
                device_id_type=MESH,
            ).start()
            return c

        lax.fori_loop(1, NE, body, 0)
        pltpu.make_async_copy(dxs.at[e, pl.ds(pl.multiple_of(16 * me, 16), 16)], back.at[e, me], ld_sem.at[2]).wait()

    def wait_back(e):
        part = back.at[e, pl.ds(0, NE - 1)]
        pltpu.make_async_copy(part, part, bk_s.at[e]).wait()
        pltpu.make_async_copy(part, part, bk_r.at[e]).wait()

    chunks = [("d", 0), ("d", 1), ("g", 0), ("u", 0), ("g", 1), ("u", 1)]

    def partial(m, quarter, put):
        kind, e = chunks[m]

        def body(i, c):
            rows = pl.ds(pl.multiple_of(i * 256, 256), 256)
            cols = pl.ds(pl.multiple_of(quarter * 512 + i * 256, 256), 256)
            a = (us if kind == "d" else xs)[e, :, cols]
            b = wh[e] if kind == "d" else dgu[e, 0 if kind == "g" else 1]
            put(i, rows, dot_tn(a, b))
            return c

        lax.fori_loop(0, 2, body, 0)

    def sa_copy(m, d):
        return pltpu.make_async_remote_copy(
            src_ref=sa.at[m % 2, pl.ds(256 * d, 256)],
            dst_ref=ra.at[m, d],
            send_sem=sa_s.at[m, d],
            recv_sem=ra_r.at[m, d],
            device_id=((right, left)[d], me),
            device_id_type=MESH,
        )

    def sb_copy(m, d):
        return pltpu.make_async_remote_copy(
            src_ref=sb.at[m % 2, d],
            dst_ref=rb.at[m, d],
            send_sem=sb_s.at[m, d],
            recv_sem=rb_r.at[m, d],
            device_id=((right, left)[d], me),
            device_id_type=MESH,
        )

    def step_a(m):
        if m >= 2:
            for d in range(2):
                sa_copy(m - 2, d).wait_send()

        def put(i, rows, value):
            sa[m % 2, rows, :] = value.astype(BF)

        partial(m, lax.rem(x + 2, NX), put)
        for d in range(2):
            sa_copy(m, d).start()

    def step_b(m):
        if m >= 2:
            for d in range(2):
                sb_copy(m - 2, d).wait_send()
        for d in range(2):
            sa_copy(m, d).wait_recv()

            def put(i, rows, value):
                add = jnp.where(i == d, ra[m, d].astype(F32), 0.0)
                sb[m % 2, d, rows, :] = (value + add).astype(BF)

            partial(m, (right, left)[d], put)
            sb_copy(m, d).start()

    outs = {"d": gd, "g": gg, "u": gu}

    def out_copy(m):
        kind, e = chunks[m]
        return pltpu.make_async_copy(outd if kind == "d" else outv.at[m % 2], outs[kind].at[e], out_sem.at[m])

    def own_part(m):
        def put(i, rows, value):
            own[rows, :] = value

        partial(m, x, put)

    def final(m):
        kind, e = chunks[m]
        own_part(m)
        if m == 1:
            out_copy(0).wait()
        if m >= 4:
            out_copy(m - 2).wait()
        for d in range(2):
            sb_copy(m, d).wait_recv()
            pltpu.make_async_copy(rb.at[m, d], rbv.at[d], ld_sem.at[d]).start()
        for d in range(2):
            pltpu.make_async_copy(rb.at[m, d], rbv.at[d], ld_sem.at[d]).wait()

        def body(i, c):
            rows = pl.ds(pl.multiple_of(i * 128, 128), 128)
            total = own[rows, :] + rbv[0, rows, :].astype(F32) + rbv[1, rows, :].astype(F32)
            if kind == "d":
                outd[:, rows] = total.T.astype(BF)
            else:
                outv[m % 2, rows, :] = total.astype(BF)
            return c

        lax.fori_loop(0, 4, body, 0)
        out_copy(m).start()

    def combine():
        rank = tab[:, 0:64]
        dvals = jnp.zeros((128, 64), F32)
        for half in range(2):
            wait_back(half)
            load = pltpu.make_async_copy(back.at[half], bkv, ld_sem.at[3])
            load.start()
            spread = jnp.where(iota((64, 512), 0) == 2 * (iota((64, 512), 1) // 16) + half, 1.0, 0.0).astype(BF)
            wide = dot(rank, spread)
            lane = iota((128, 512), 1) % 16
            pm = jnp.where(wide == (lane + 1).astype(F32), 1.0, 0.0).astype(BF)
            load.wait()
            for n in range(4):
                cols = slice(512 * n, 512 * n + 512)
                got = dot(pm, bkv[:, :, cols].reshape(512, 512))
                tokacc[:, cols] = got if half == 0 else tokacc[:, cols] + got
            over = bkv[:, :, D : D + 256].reshape(512, 256)
            info = bkv[:, :, D + 256 :].reshape(512, 128).astype(F32)
            own_expert = iota((512, 64), 1) == 2 * (iota((512, 64), 0) // 16) + half
            for q in range(8):
                po = jnp.where((wide == (17 + lane // 8).astype(F32)) & (lane % 8 == q), 1.0, 0.0).astype(BF)
                cols = slice(256 * q, 256 * q + 256)
                tokacc[:, cols] = tokacc[:, cols] + dot(po, over)
                if q == 0:
                    dvals = dvals + dot(po, jnp.where(own_expert, info[:, 1:2], 0.0).astype(BF))
            dvals = dvals + dot(pm, jnp.where(own_expert, info[:, 0:1], 0.0).astype(BF))
        gtok[...] = tokacc[...].astype(BF)
        expert = iota((128, 64), 1)
        picked = [
            jnp.sum(jnp.where(ids[:, k : k + 1] == expert, dvals, 0.0), axis=1, keepdims=True) for k in range(8)
        ]
        dgate = jnp.concatenate(picked, axis=1)
        pr = probs[...]
        glog[...] = pr * (dgate - jnp.sum(pr * dgate, axis=1, keepdims=True))

    forward(0)
    start_weights(1)
    dispatch(ug, us, False)
    step_a(0)
    forward(1)
    start_weights(0)
    step_a(1)
    step_b(0)
    backward(0)
    step_a(2)
    step_b(1)
    backward(1)
    final(0)
    step_a(3)
    step_b(2)
    input_grad(0)
    start_weights(1)
    send_back(0)
    input_grad(1)
    send_back(1)
    final(1)
    step_a(4)
    step_b(3)
    final(2)
    step_a(5)
    step_b(4)
    final(3)
    step_b(5)
    final(4)
    combine()
    final(5)
    for m in (4, 5):
        for d in range(2):
            sa_copy(m, d).wait_send()
            sb_copy(m, d).wait_send()
    for m in (1, 4, 5):
        out_copy(m).wait()


def on_device(tokens, expert_ids, gate_logits, upstream, w_gate, w_up, w_down):
    probs = jax.nn.softmax(gate_logits, axis=-1)
    tab = routing_table(expert_ids, probs.astype(BF).astype(F32))
    tg = lax.all_gather(jnp.concatenate([tokens, tab], axis=1), "expert").reshape(16, 256, D + 128)
    ug = lax.all_gather(upstream, "expert").reshape(16, 256, D)
    sd = jax.ShapeDtypeStruct
    dma = pltpu.SemaphoreType.DMA
    vm = pltpu.VMEM
    res = pl.pallas_call(
        kernel,
        out_shape=(
            sd((128, D), BF),
            sd((128, 8), F32),
            sd((2, 512, FF), BF),
            sd((2, 512, FF), BF),
            sd((2, FF, 512), BF),
            sd((6, 2, 512, FF), BF),
            sd((2, NE, 16, BACK), BF),
        ),
        in_specs=[ANY] * 5 + [VMEM] * 3,
        out_specs=(VMEM, VMEM, ANY, ANY, ANY, ANY, ANY),
        scratch_shapes=[
            vm((2, 256, D + 128), BF),
            vm((16, 80, 256), BF),
            vm((2, ROWS, D), BF),
            vm((2, ROWS, D), BF),
            vm((128, D + 128), F32),
            vm((2, ROWS, 128), F32),
            vm((D, FF), BF),
            vm((D, FF), BF),
            vm((FF, D), BF),
            vm((2, ROWS, FF), F32),
            vm((2, ROWS, FF), F32),
            vm((2, ROWS, FF), BF),
            vm((2, 2, ROWS, FF), BF),
            vm((2, ROWS, 128), F32),
            vm((2, 512, FF), BF),
            vm((6, 2, 256, FF), BF),
            vm((2, 2, 512, FF), BF),
            vm((2, 512, FF), BF),
            vm((512, FF), F32),
            vm((2, 512, FF), BF),
            vm((FF, 512), BF),
            vm((2, ROWS, BACK), BF),
            vm((NE, 16, BACK), BF),
            vm((128, D), F32),
            dma((2,)),
            dma((3,)),
            dma((6, 2)),
            dma((6, 2)),
            dma((6, 2)),
            dma((6, 2)),
            dma((2,)),
            dma((2,)),
            dma((4,)),
            dma((6,)),
        ],
        compiler_params=pltpu.CompilerParams(collective_id=0, has_side_effects=True, vmem_limit_bytes=64 << 20),
        cost_estimate=pl.CostEstimate(flops=29 * 10**9, bytes_accessed=10**8, transcendentals=10**6),
        name="expert_backward",
    )(tg, ug, w_gate, w_up, w_down, tab, expert_ids, probs)
    return res[:5]


def solution(mesh):
    rows = P(("dp", "expert"), None)
    whole = P("expert", None, None)
    return jax.shard_map(
        on_device,
        mesh=mesh,
        in_specs=(rows, rows, rows, rows, whole, whole, whole),
        out_specs=(rows, rows, P("expert", "dp", None), P("expert", "dp", None), P("expert", None, "dp")),
        check_vma=False,
    )
```

time: 430 us -> 380 us (0.88); the launches traced: 422 us -> 379 us
  Pallas kernels: 0 us -> 200 us
  matrix products: 107 us -> 0.35 us
  local copies, waits for them, and re-layouts: 107 us -> 13.2 us
  starting transfers between devices: 43.6 us -> 0.08 us
  waiting for transfers between devices: 122 us -> 148 us
  other arithmetic: 27.1 us -> 3.27 us
    pallas_call x0 -> x1, Pallas kernels: none -> 200 us  [on_device(): pl.pallas_call(kernel, out_shape=(sd((128, D), BF), sd((128, 8), F32), sd...]
    all_gather x0 -> x2, waiting for transfers between devices: none -> 148 us  [the longest x1 77.3 us: on_device(): lax.all_gather(jnp.concatenate([tokens, tab], axis=1), 'expert')]
    all_to_all x5 -> x0, waiting for transfers between devices: 114 us -> none  [the longest x1 47.8 us: on_device(): lax.all_to_all(slot_dx.reshape(send_shape), 'expert', split_axis=1, conca...]
    dot_general x8 -> x1, matrix products: 107 us -> 0.35 us  [dot(): return jnp.dot(a, b, preferred_element_type=F32)]
    reshape x10 -> x0, local copies, waits for them, and re-layouts: 43.9 us -> none  [the longest x2 17.5 us: on_device(): jnp.concatenate([tokens, zero_row], axis=0)[slot_token].reshape(send_shape)]
    all_to_all x5 -> x0, starting transfers between devices: 43.2 us -> none  [the longest x1 9.6 us: on_device(): lax.all_to_all(gate_send, 'expert', split_axis=1, concat_axis=1, tiled=True)]
    gather x5 -> x0, local copies, waits for them, and re-layouts: 37.9 us -> none  [the longest x1 11.8 us: on_device(): back_dx.reshape(slot_count, width)[slot_index]]
    another operation x3 -> x1, other arithmetic: 18.2 us -> 0.34 us
  transfers between devices with their start and end apart: 8 -> 2, of which waited for: 4 -> 2; matrix products, arithmetic and copies ran while one was open for 46% -> 2% of each run, Pallas kernels for 0% -> 0%
where the time goes in v1:
time: 380 us; the launch traced here: 379 us
  Pallas kernels  200 us (53%)
  waiting for transfers between devices  148 us (39%)
  between operations  14.1 us (4%)
  local copies, waits for them, and re-layouts  13.2 us (3%)
    pallas_call x1, Pallas kernels, on_device(): pl.pallas_call(kernel, out_shape=(sd((128, D), BF), sd((128, 8), F32), sd...  200 us
    all_gather x1, waiting for transfers between devices, on_device(): lax.all_gather(jnp.concatenate([tokens, tab], axis=1), 'expert')  77.3 us
    all_gather x1, waiting for transfers between devices, on_device(): ug = lax.all_gather(upstream, 'expert').reshape(16, 256, D)  70.2 us
    unnamed x10, local copies, waits for them, and re-layouts  9.89 us
  transfers between devices with their start and end apart: 2, of which 2 were waited for; matrix products, arithmetic and copies ran while one was open for 2% of the time, Pallas kernels for 0%

profile of v1, /device:TPU:1, one launch (start us, length us, event | category | flops | bytes accessed | tf_op | source)
XLA Modules:
  0.0 378.8 jit_solution(6243196675384507225)
XLA Ops:
  7.2 0.0 all-gather.7.cloned.1.call-start
  7.2 0.7 all-gather.7.cloned.1.call-update
  7.9 0.0 all-gather.5.cloned.1.call-start
  7.9 0.7 reduce_max.9
  8.6 0.7 broadcast_subtract_fusion
  9.3 0.1 copy.23
  9.4 0.1 exponential_reduce_fusion
  9.6 0.7 convert_convert_fusion
  10.3 0.4 slice_reduce_fusion.7
  10.7 1.0 slice_bitcast_fusion.7
  11.6 0.3 fusion.1
  12.0 0.3 add_convert_fusion
  12.4 1.8 concatenate.8
  14.2 0.0 all-gather.5.cloned.1.call-update
  14.2 1.4 copy.24.ids
  15.6 0.7 pad_maximum_fusion.tab
  16.3 70.2 %all-gather.7.cloned.1.call-done = bf16[4096,2048]{1,0:T(8,128)(2,1)} async-done(((bf16[128,2048]{1,0:T(8,128)(2,1)}), bf16[4096,2048]{1,0:T(8,128)(2,1)}) %all-gather.7.cloned.1.call-update) | async-done | bytes 16777232 | tf_op jit(solution)/shard_map/all_gather | solution.py:416
  86.5 77.3 %all-gather.5.cloned.1.call-done = bf16[4096,2176]{1,0:T(8,128)(2,1)} async-done(((bf16[128,2176]{1,0:T(8,128)(2,1)}), bf16[4096,2176]{1,0:T(8,128)(2,1)}) %all-gather.5.cloned.1.call-update) | async-done | bytes 17825808 | tf_op jit(solution)/shard_map/all_gather | solution.py:415
  163.9 199.6 %expert_backward.1 = (bf16[128,2048]{1,0:T(8,128)(2,1)}, f32[128,8]{1,0:T(8,128)}, bf16[2,512,768]{2,1,0:T(8,128)(2,1)}, bf16[2,512,768]{2,1,0:T(8,128)(2,1)}, b...) custom-call(bf16[16,256,2176]{2,1,0:T(8,128)(2,1)} %bitcast.18, ...), custom_call_target="tpu_custom_call" | custom-call | flops 28999999488 | bytes 100000000 | tf_op jit(solution)/shard_map/expert_backward/pallas_call | solution.py:420
  363.4 0.0 copy-start.1
  363.4 0.0 copy-start
  363.4 1.7 copy.25
  365.1 1.9 copy.31
  367.0 2.7 copy.32
  369.6 0.0 copy-done.1
  369.6 1.1 copy.33
  370.8 0.0 copy-done
  370.8 1.1 copy.34
Async XLA Ops:
  7.2 79.4 %all-gather.7.cloned.1.call-start = ((), (), s32[]{:S(2)}) async-start(), calls=%async_computation.1 | async-start | bytes 17301504 | tf_op jit(solution)/shard_map/all_gather | solution.py:416
  7.9 156.0 %all-gather.5.cloned.1.call-start = ((), (), s32[]{:S(2)}) async-start(), calls=%async_computation | async-start | bytes 18382848 | tf_op jit(solution)/shard_map/all_gather | solution.py:415
  363.4 6.2 %copy-start.1 = (bf16[2,512,768]{2,1,0:T(8,128)(2,1)S(1)}, bf16[2,512,768]{2,1,0:T(8,128)(2,1)}, u32[]{:S(2)}) copy-start(bf16[2,512,768]{2,1,0:T(8,128)(2,1)} %get-tuple-element.56) | copy-start | bytes 4718596
  363.4 7.3 %copy-start = (bf16[2,768,512]{2,1,0:T(8,128)(2,1)S(1)}, bf16[2,768,512]{2,1,0:T(8,128)(2,1)}, u32[]{:S(2)}) copy-start(bf16[2,768,512]{2,1,0:T(8,128)(2,1)} %get-tuple-element.57) | copy-start | bytes 4718596
Sparse Core Ops, SparseCore 0:
  10.3 76.2 all-gather.6
  89.4 74.4 all-gather.4

commit v2 on v1

--- a/solution.py
+++ b/solution.py
@@ -55,15 +55,20 @@
     return jnp.where(ok, slot + 1, -1).astype(F32), jnp.where(second, 1.0, 0.0)
 
 
+JOBS = ((1152, 1024), (256, 256), (512, 512), (256, 256))
+
+
 def kernel(
-    tg, ug, wg, wu, wd, tab, ids, probs,
-    gtok, glog, gg, gu, gd, rb, back,
-    stage, pmat, xs, us, ov, xgate, wgv, wuv, wdv, pre_g, pre_u, wh, dgu, dgacc,
+    tokens, upstream, wg, wu, wd, ids, logits,
+    gtok, glog, gg, gu, gd, rb, back, g00, g01, g10, g11, g20, g21, g30, g31,
+    tab, first, stage, pmat, xs, us, ov, xgate, wgv, wuv, wdv, pre_g, pre_u, wh, dgu, dgacc,
     sa, ra, sb, rbv, own, outv, outd, dxs, bkv, tokacc,
-    stage_sem, w_sem, sa_s, ra_r, sb_s, rb_r, bk_s, bk_r, ld_sem, out_sem,
+    ag_s, ag_r, ag_l, stage_sem, w_sem, sa_s, ra_r, sb_s, rb_r, bk_s, bk_r, ld_sem, out_sem,
 ):
+    gathered = ((g00, g01), (g10, g11), (g20, g21), (g30, g31))
     x, me = lax.axis_index("dp"), lax.axis_index("expert")
     right, left = lax.rem(x + 1, NX), lax.rem(x + 3, NX)
+    z, y, core = me // 8, (me // 2) % 4, me % 2
 
     barrier = pltpu.get_barrier_semaphore()
 
@@ -91,59 +96,185 @@
     start_weights(0)
     wdload(0).start()
 
+    def place(r, a, b):
+        return (b, a) if r == 0 else (a, b)
+
+    def peer(r, a, b):
+        pz, py = place(r, a % 4, b % 4)
+        return (pz * 4 + py) * 2 + core
+
+    pos = ((y, z), (z, y))
+
+    def chunk(j, r, b, half=None):
+        g = gathered[j][r]
+        span = pl.ds(0, 4) if half is None else pl.ds(2 * half, 2)
+        return g.at[b % 4, span, core] if r == 0 else g.at[span, b % 4, core]
+
+    def block(j, r, a):
+        pz, py = place(r, a % 4, pos[r][1])
+        return gathered[j][r].at[pz, py, core]
+
+    def source(j, r):
+        if j == 0:
+            return first if r == 0 else tokens.at[:, pl.ds(1024, 1024)]
+        if j == 2:
+            return upstream.at[:, pl.ds(pl.multiple_of(512 * (right, left)[r], 512), 512)]
+        quarter = lax.rem(x + 2, NX) if j == 1 else x
+        return upstream.at[:, pl.ds(pl.multiple_of(512 * quarter + 256 * r, 256), 256)]
+
+    def ag(j, r, k):
+        p1, p2 = pos[r]
+        if k < 2:
+            src, dst = source(j, r), block(j, r, p1)
+        elif k < 4:
+            rows = pl.ds(64 * (k - 2), 64)
+            src = dst = block(j, r, p1 + (3, 1)[k - 2]).at[rows]
+        elif k < 6:
+            src = dst = chunk(j, r, p2)
+        elif k < 8:
+            src = dst = chunk(j, r, p2 + (3, 1)[k - 6], half=k - 6)
+        else:
+            src = dst = chunk(j, r, p2 + (0, 3, 1, 2)[k - 8])
+        if k < 4:
+            to = peer(r, p1 + (1, 3)[k % 2], p2)
+        elif k < 8:
+            to = peer(r, p1, p2 + (1, 3)[k % 2])
+        else:
+            to = (z * 4 + y) * 2 + 1 - core
+        return pltpu.make_async_remote_copy(
+            src_ref=src,
+            dst_ref=dst,
+            send_sem=ag_s.at[j, r, k],
+            recv_sem=ag_r.at[j, r, k],
+            device_id=(x, to),
+            device_id_type=MESH,
+        )
+
+    def keep(j, r):
+        return pltpu.make_async_copy(source(j, r), block(j, r, pos[r][0]), ag_l.at[j, r])
+
+    def ag_own(j):
+        for r in range(2):
+            ag(j, r, 0).start()
+            ag(j, r, 1).start()
+            keep(j, r).start()
+
+    def ag_ring(j):
+        for r in range(2):
+            for k in range(2):
+                ag(j, r, k).wait_recv()
+                ag(j, r, k + 2).start()
+
+    def ag_chunk(j):
+        for r in range(2):
+            ag(j, r, 2).wait_recv()
+            ag(j, r, 3).wait_recv()
+            keep(j, r).wait()
+            for k in (4, 5, 8):
+                ag(j, r, k).start()
+
+    def ag_forward(j):
+        for r in range(2):
+            for k in range(2):
+                ag(j, r, k + 4).wait_recv()
+                ag(j, r, k + 6).start()
+                ag(j, r, k + 9).start()
+
+    def ag_last(j):
+        for r in range(2):
+            ag(j, r, 6).wait_recv()
+            ag(j, r, 7).wait_recv()
+            ag(j, r, 11).start()
+
     target, second = slot_targets()
 
-    def dispatch(src, dst, table):
-        w = src.shape[2]
-
-        def load(j, slot):
-            return pltpu.make_async_copy(src.at[j], stage.at[slot, :, pl.ds(0, w)], stage_sem.at[slot])
-
-        load(0, 0).start()
-
-        def body(j, c):
-            slot = lax.rem(j, 2)
-
-            @pl.when(j + 1 < 16)
-            def _():
-                load(j + 1, 1 - slot).start()
-
-            load(j, slot).wait()
-            if table:
-                tabj = stage[slot, :, D : D + 128]
+    def load(j, r, b, slot):
+        g = gathered[j][r]
+        src = g.at[b] if r == 0 else g.at[:, b]
+        return pltpu.make_async_copy(src, stage.at[slot, :, :, :, pl.ds(0, JOBS[j][r])], stage_sem.at[slot])
+
+    def column(j, r):
+        if j == 0:
+            return 1024 * r
+        if j == 2:
+            return pl.multiple_of(512 * (right, left)[r], 512)
+        return pl.multiple_of(512 * (lax.rem(x + 2, NX) if j == 1 else x) + 256 * r, 256)
+
+    def pieces(j, r):
+        w = JOBS[j][r]
+        return [(at, min(512, w - at)) for at in range(0, w, 512)]
+
+    def multiply(j, r, b, slot):
+        dst = xs if j == 0 else us
+        base = column(j, r)
+
+        def body(k, c):
+            pz, py = place(r, k, b)
+            chip = pz * 4 + py
+            at = pl.multiple_of(32 * chip, 32)
+            at8 = pl.multiple_of(8 * chip, 8)
+            if j == 0 and r == 0:
+                tabj = stage[slot, k, :, :, 1024:1152].reshape(256, 128)
                 pick = jnp.where(iota((8, 128), 1) == 2 * me + iota((8, 128), 0), 1.0, 0.0).astype(BF)
                 ranks = dot_nt(pick, tabj)
                 row0 = jnp.broadcast_to(ranks[0:1, :], (80, 256))
                 row1 = jnp.broadcast_to(ranks[1:2, :], (80, 256))
                 pm = jnp.where(jnp.where(second > 0.5, row1, row0) == target, 1.0, 0.0).astype(BF)
-                pmat[j] = pm
+                pmat[chip] = pm
                 got = dot(pm, tabj)
-                at = pl.multiple_of(32 * j, 32)
                 xgate[0, pl.ds(at, 32), :] = got[0:32]
                 xgate[1, pl.ds(at, 32), :] = got[32:64]
-                ov[pl.ds(pl.multiple_of(8 * j, 8), 8), D : D + 128] = got[64:72]
-            pm = pmat[j]
-            for n in range(D // 512):
-                cols = slice(512 * n, 512 * n + 512)
-                got = dot(pm, stage[slot, :, cols])
-                at = pl.multiple_of(32 * j, 32)
+                ov[pl.ds(at8, 8), D : D + 128] = got[64:72]
+            pm = pmat[chip]
+            for off, w in pieces(j, r):
+                if w == 128:
+                    continue
+                got = dot(pm, stage[slot, k, :, :, off : off + w].reshape(256, w))
+                cols = pl.ds(base + off, w)
                 dst[0, pl.ds(at, 32), cols] = got[0:32].astype(BF)
                 dst[1, pl.ds(at, 32), cols] = got[32:64].astype(BF)
-                ov[pl.ds(pl.multiple_of(8 * j, 8), 8), cols] = got[64:72]
-            return c
-
-        lax.fori_loop(0, 16, body, 0)
-        r, col = iota((64, 128), 0), iota((64, 128), 1)
+                ov[pl.ds(at8, 8), cols] = got[64:72]
+            return c
+
+        lax.fori_loop(0, 4, body, 0)
+
+    def overflow(j, r):
+        dst = xs if j == 0 else us
+        row, col = iota((64, 128), 0), iota((64, 128), 1)
         for e in range(2):
-            sel = jnp.where(col == 8 * (r // 4) + 4 * e + r % 4, 1.0, 0.0).astype(BF)
-            for n in range(D // 512):
-                cols = slice(512 * n, 512 * n + 512)
+            sel = jnp.where(col == 8 * (row // 4) + 4 * e + row % 4, 1.0, 0.0).astype(BF)
+            for off, w in pieces(j, r):
+                if w == 128:
+                    xgate[e, 512:576, :] = dot(sel, ov[:, D : D + 128].astype(BF))
+                    continue
+                cols = pl.ds(column(j, r) + off, w)
                 dst[e, 512:576, cols] = dot(sel, ov[:, cols].astype(BF)).astype(BF)
-            if table:
-                xgate[e, 512:576, :] = dot(sel, ov[:, D : D + 128].astype(BF))
-
-    dispatch(tg, xs, True)
-    pl.semaphore_wait(barrier, NE - 1 + 2)
+
+    def dispatch_one(j, r, n):
+        b = (pos[r][1] + (0, 3, 1, 2)[n]) % 4
+        ag(j, r, 8 + n).wait_recv()
+        load(j, r, b, 0).start()
+        load(j, r, b, 0).wait()
+        multiply(j, r, b, 0)
+
+    def dispatch(j, r):
+        for n in range(4):
+            ag(j, r, 8 + n).wait_recv()
+        load(j, r, 0, 0).start()
+
+        def body(b, c):
+            slot = lax.rem(b, 2)
+
+            @pl.when(b < 3)
+            def _():
+                load(j, r, b + 1, 1 - slot).start()
+
+            load(j, r, b, slot).wait()
+            multiply(j, r, b, slot)
+            return c
+
+        lax.fori_loop(0, 4, body, 0)
+        overflow(j, r)
 
     def gate_of(e, rows):
         lane = iota((rows.size, 128), 1)
@@ -367,20 +498,59 @@
             jnp.sum(jnp.where(ids[:, k : k + 1] == expert, dvals, 0.0), axis=1, keepdims=True) for k in range(8)
         ]
         dgate = jnp.concatenate(picked, axis=1)
-        pr = probs[...]
-        glog[...] = pr * (dgate - jnp.sum(pr * dgate, axis=1, keepdims=True))
-
+        glog[...] = probs * (dgate - jnp.sum(probs * dgate, axis=1, keepdims=True))
+
+    left_half = pltpu.make_async_copy(tokens.at[:, pl.ds(0, 1024)], first.at[:, pl.ds(0, 1024)], ld_sem.at[3])
+    left_half.start()
+    raised = jnp.exp(logits[...] - jnp.max(logits[...], axis=1, keepdims=True))
+    probs = raised / jnp.sum(raised, axis=1, keepdims=True)
+    tab[...] = routing_table(ids[...], probs.astype(BF).astype(F32))
+    first[:, 1024:1152] = tab[...]
+    left_half.wait()
+    pl.semaphore_wait(barrier, NE - 1 + 2)
+
+    ag_own(0)
+    ag_ring(0)
+    ag_chunk(0)
+    ag_own(1)
+    dispatch_one(0, 0, 0)
+    ag_ring(1)
+    ag_forward(0)
+    ag_chunk(1)
+    dispatch_one(0, 0, 1)
+    dispatch_one(0, 0, 2)
+    ag_last(0)
+    ag_own(2)
+    ag_forward(1)
+    dispatch_one(0, 0, 3)
+    overflow(0, 0)
+    dispatch(0, 1)
+    ag_ring(2)
+    ag_chunk(2)
     forward(0)
     start_weights(1)
-    dispatch(ug, us, False)
+    ag_last(1)
+    dispatch(1, 0)
+    dispatch(1, 1)
     step_a(0)
+    ag_own(3)
+    ag_ring(3)
+    ag_forward(2)
     forward(1)
     start_weights(0)
     step_a(1)
+    ag_chunk(3)
+    ag_last(2)
+    dispatch(2, 0)
+    dispatch(2, 1)
     step_b(0)
+    ag_forward(3)
+    step_b(1)
+    ag_last(3)
+    dispatch(3, 0)
+    dispatch(3, 1)
     backward(0)
     step_a(2)
-    step_b(1)
     backward(1)
     final(0)
     step_a(3)
@@ -407,13 +577,13 @@
             sb_copy(m, d).wait_send()
     for m in (1, 4, 5):
         out_copy(m).wait()
+    for j in range(4):
+        for r in range(2):
+            for k in range(12):
+                ag(j, r, k).wait_send()
 
 
 def on_device(tokens, expert_ids, gate_logits, upstream, w_gate, w_up, w_down):
-    probs = jax.nn.softmax(gate_logits, axis=-1)
-    tab = routing_table(expert_ids, probs.astype(BF).astype(F32))
-    tg = lax.all_gather(jnp.concatenate([tokens, tab], axis=1), "expert").reshape(16, 256, D + 128)
-    ug = lax.all_gather(upstream, "expert").reshape(16, 256, D)
     sd = jax.ShapeDtypeStruct
     dma = pltpu.SemaphoreType.DMA
     vm = pltpu.VMEM
@@ -427,11 +597,14 @@
             sd((2, FF, 512), BF),
             sd((6, 2, 512, FF), BF),
             sd((2, NE, 16, BACK), BF),
+            *[sd((4, 4, 2, 128, w), BF) for pair in JOBS for w in pair],
         ),
-        in_specs=[ANY] * 5 + [VMEM] * 3,
-        out_specs=(VMEM, VMEM, ANY, ANY, ANY, ANY, ANY),
+        in_specs=[ANY] * 5 + [VMEM] * 2,
+        out_specs=(VMEM, VMEM) + (ANY,) * 13,
         scratch_shapes=[
-            vm((2, 256, D + 128), BF),
+            vm((128, 128), BF),
+            vm((128, 1152), BF),
+            vm((2, 4, 2, 128, 1152), BF),
             vm((16, 80, 256), BF),
             vm((2, ROWS, D), BF),
             vm((2, ROWS, D), BF),
@@ -455,6 +628,9 @@
             vm((2, ROWS, BACK), BF),
             vm((NE, 16, BACK), BF),
             vm((128, D), F32),
+            dma((4, 2, 12)),
+            dma((4, 2, 12)),
+            dma((4, 2)),
             dma((2,)),
             dma((3,)),
             dma((6, 2)),
@@ -469,7 +645,7 @@
         compiler_params=pltpu.CompilerParams(collective_id=0, has_side_effects=True, vmem_limit_bytes=64 << 20),
         cost_estimate=pl.CostEstimate(flops=29 * 10**9, bytes_accessed=10**8, transcendentals=10**6),
         name="expert_backward",
-    )(tg, ug, w_gate, w_up, w_down, tab, expert_ids, probs)
+    )(tokens, upstream, w_gate, w_up, w_down, expert_ids, gate_logits)
     return res[:5]
 
 

time: 380 us -> 290 us (0.76)
  waiting for transfers between devices: 148 us -> 0 us
  Pallas kernels: 200 us -> 276 us
  between operations: 14.1 us -> 0.64 us
    all_gather x2 -> x0, waiting for transfers between devices: 148 us -> none  [the longest x1 77.3 us: on_device(): lax.all_gather(jnp.concatenate([tokens, tab], axis=1), 'expert')]
    pallas_call x1, Pallas kernels: 200 us -> 276 us  [on_device(): pl.pallas_call(kernel, out_shape=(sd((128, D), BF), sd((128, 8), F32), sd...]
    unnamed x10 -> x11, local copies, waits for them, and re-layouts: 9.89 us -> 12.1 us
  transfers between devices with their start and end apart: 2 -> 0, of which waited for: 2 -> 0; matrix products, arithmetic and copies ran while one was open for 2% -> 0% of each run, Pallas kernels for 0% -> 0%
where the time goes in v2:
time: 290 us; the launch traced here: 289 us
  Pallas kernels  276 us (95%)
  local copies, waits for them, and re-layouts  12.1 us (4%)
    pallas_call x1, Pallas kernels, on_device(): pl.pallas_call(kernel, out_shape=(sd((128, D), BF), sd((128, 8), F32), sd...  276 us
    unnamed x11, local copies, waits for them, and re-layouts  12.1 us

profile of v2, /device:TPU:1, one launch (start us, length us, event | category | flops | bytes accessed | tf_op | source)
XLA Modules:
  0.0 289.0 jit_solution(12612390520980737436)
XLA Ops:
  0.6 1.4 copy.12.ids
  2.0 1.4 copy.13.logits
  3.5 276.3 %expert_backward.1 = (bf16[128,2048]{1,0:T(8,128)(2,1)}, f32[128,8]{1,0:T(8,128)}, bf16[2,512,768]{2,1,0:T(8,128)(2,1)}, bf16[2,512,768]{2,1,0:T(8,128)(2,1)}, b...) custom-call(bf16[128,2048]{1,0:T(8,128)(2,1)} %tokens.1, ...), custom_call_target="tpu_custom_call" | custom-call | flops 28999999488 | bytes 100000000 | tf_op jit(solution)/shard_map/expert_backward/pallas_call | solution.py:590
  279.7 1.5 copy.14
  281.2 0.0 copy-start.1
  281.2 2.0 copy.19
  283.2 2.7 copy.20
  285.9 0.0 copy-done.1
  285.9 0.0 copy-start
  285.9 1.1 copy.21
  287.0 0.8 copy-done
  287.9 1.1 copy.22
Async XLA Ops:
  281.2 4.7 %copy-start.1 = (bf16[2,512,768]{2,1,0:T(8,128)(2,1)S(1)}, bf16[2,512,768]{2,1,0:T(8,128)(2,1)}, u32[]{:S(2)}) copy-start(bf16[2,512,768]{2,1,0:T(8,128)(2,1)} %get-tuple-element.28) | copy-start | bytes 4718596
  285.9 2.0 copy-start

commit v3 on v2

v3 whole, which is shorter than its diff:
```python
import jax
import jax.numpy as jnp
from jax import lax
from jax.experimental import pallas as pl
from jax.experimental.pallas import tpu as pltpu
from jax.sharding import PartitionSpec as P

MESH = pl.DeviceIdType.MESH
BF = jnp.bfloat16
F32 = jnp.float32
D, FF, NE, NX = 2048, 768, 32, 4
MAIN, OVF = 16, 2
ROWS = NE * (MAIN + OVF)
BACK = D + 256 + 128
ANY = pl.BlockSpec(memory_space=pl.ANY)
VMEM = pl.BlockSpec(memory_space=pltpu.VMEM)


def iota(shape, dim):
    return lax.broadcasted_iota(jnp.int32, shape, dim)


def dot_nt(a, b):
    return lax.dot_general(a, b, (((1,), (1,)), ((), ())), preferred_element_type=F32)


def dot_tn(a, b):
    return lax.dot_general(a, b, (((0,), (0,)), ((), ())), preferred_element_type=F32)


def dot(a, b):
    return jnp.dot(a, b, preferred_element_type=F32)


def slot_numbers(ids):
    expert = iota((128, 64), 1)
    routed = jnp.zeros((128, 64), F32)
    for k in range(8):
        routed = routed + jnp.where(ids[:, k : k + 1] == expert, 1.0, 0.0)
    before = jnp.where(iota((128, 128), 1) < iota((128, 128), 0), 1.0, 0.0)
    rank = dot(before.astype(BF), routed.astype(BF))
    return jnp.where(routed > 0, rank + 1.0, 0.0).astype(BF)


def slot_targets():
    row, lane = iota((80, 256), 0), iota((80, 256), 1)
    over = row - 64
    core = jnp.where(row < 64, (row % 32) // 16, (over % 4) // 2)
    slot = jnp.where(row < 64, row % 16, 16 + over % 2)
    ok = (core == lane // 128) & (row < 72)
    second = ((row >= 32) & (row < 64)) | (over >= 4)
    return jnp.where(ok, slot + 1, -1).astype(F32), jnp.where(second, 1.0, 0.0)


JOBS = (1024, 256, 256, 256, 256)
NJ = len(JOBS)


def kernel(
    tokens, upstream, wg, wu, wd, ids, logits,
    gtok, glog, gg, gu, gd, rb, back, g00, g01, g10, g11, g20, g21, g30, g31, g40, g41,
    meta, metas, ranks, stage, pmat, xs, us, ov, xgate, wgv, wuv, wdv, pre_g, pre_u, wh, dgu, dgacc,
    sa, ra, sb, rbv, own, outv, outd, dxs, tokacc,
    mt_s, mt_r, ag_s, ag_r, ag_l, stage_sem, w_sem, sa_s, ra_r, sb_s, rb_r, bk_s, bk_r, bk_l, ld_sem, out_sem,
):
    gathered = ((g00, g01), (g10, g11), (g20, g21), (g30, g31), (g40, g41))
    x, me = lax.axis_index("dp"), lax.axis_index("expert")
    right, left = lax.rem(x + 1, NX), lax.rem(x + 3, NX)
    z, y, core = me // 8, (me // 2) % 4, me % 2

    barrier = pltpu.get_barrier_semaphore()

    def greet(i, c):
        pl.semaphore_signal(barrier, inc=1, device_id=(x, lax.rem(me + i, NE)), device_id_type=MESH)
        return c

    lax.fori_loop(1, NE, greet, 0)
    for other in (right, left):
        pl.semaphore_signal(barrier, inc=1, device_id=(other, me), device_id_type=MESH)

    def wload(e):
        return [
            pltpu.make_async_copy(wg.at[e], wgv, w_sem.at[0]),
            pltpu.make_async_copy(wu.at[e], wuv, w_sem.at[1]),
        ]

    def wdload(e):
        return pltpu.make_async_copy(wd.at[e], wdv, w_sem.at[2])

    def start_weights(e):
        for cp in wload(e):
            cp.start()

    def place(r, a, b):
        return (b, a) if r == 0 else (a, b)

    def peer(r, a, b):
        pz, py = place(r, a % 4, b % 4)
        return (pz * 4 + py) * 2 + core

    pos = ((y, z), (z, y))

    def chunk(j, r, b, half=None):
        g = gathered[j][r]
        span = pl.ds(0, 4) if half is None else pl.ds(2 * half, 2)
        return g.at[b % 4, span, core] if r == 0 else g.at[span, b % 4, core]

    def block(j, r, a):
        pz, py = place(r, a % 4, pos[r][1])
        return gathered[j][r].at[pz, py, core]

    def column(j, r):
        if j == 0:
            return 1024 * r
        quarter = (lax.rem(x + 2, NX), (right, left)[r], (right, left)[r], x)[j - 1]
        return pl.multiple_of(512 * quarter + (256 * r, 0, 256, 256 * r)[j - 1], 256)

    def source(j, r):
        return dxs.at[min(j, 1), pl.ds(0, 128), pl.ds(column(j, r), JOBS[j])]

    def ag(j, r, k):
        p1, p2 = pos[r]
        if k < 2:
            src, dst = source(j, r), block(j, r, p1)
        elif k < 4:
            rows = pl.ds(64 * (k - 2), 64)
            src = dst = block(j, r, p1 + (3, 1)[k - 2]).at[rows]
        elif k < 6:
            src = dst = chunk(j, r, p2)
        elif k < 8:
            src = dst = chunk(j, r, p2 + (3, 1)[k - 6], half=k - 6)
        else:
            src = dst = chunk(j, r, p2 + (0, 3, 1, 2)[k - 8])
        if k < 4:
            to = peer(r, p1 + (1, 3)[k % 2], p2)
        elif k < 8:
            to = peer(r, p1, p2 + (1, 3)[k % 2])
        else:
            to = (z * 4 + y) * 2 + 1 - core
        return pltpu.make_async_remote_copy(
            src_ref=src,
            dst_ref=dst,
            send_sem=ag_s.at[j, r, k],
            recv_sem=ag_r.at[j, r, k],
            device_id=(x, to),
            device_id_type=MESH,
        )

    def keep(j, r):
        return pltpu.make_async_copy(source(j, r), block(j, r, pos[r][0]), ag_l.at[j, r])

    def ag_own(j):
        for r in range(2):
            ag(j, r, 0).start()
            ag(j, r, 1).start()
            keep(j, r).start()

    def ag_ring(j):
        for r in range(2):
            for k in range(2):
                ag(j, r, k).wait_recv()
                ag(j, r, k + 2).start()

    def ag_chunk(j):
        for r in range(2):
            ag(j, r, 2).wait_recv()
            ag(j, r, 3).wait_recv()
            keep(j, r).wait()
            for k in (4, 5, 8):
                ag(j, r, k).start()

    def ag_forward(j):
        for r in range(2):
            for k in range(2):
                ag(j, r, k + 4).wait_recv()
                ag(j, r, k + 6).start()
                ag(j, r, k + 9).start()

    def ag_last(j):
        for r in range(2):
            ag(j, r, 6).wait_recv()
            ag(j, r, 7).wait_recv()
            ag(j, r, 11).start()

    target, second = slot_targets()

    def order(r, n):
        return (pos[r][1] + (0, 3, 1, 2)[n]) % 4

    def load(j, r, n):
        g = gathered[j][r]
        b = order(r, n)
        part = (n % 2, 0, 1024) if j == 0 else ((j - 1) % 2, 256 * n, 256)
        src = g.at[b] if r == 0 else g.at[:, b]
        return pltpu.make_async_copy(
            src, stage.at[part[0], r, :, :, :, pl.ds(part[1], part[2])], stage_sem.at[part[0], r, 0 if j == 0 else n]
        )

    def fetch(j, n):
        for r in range(2):
            ag(j, r, 8 + n).wait_recv()
            load(j, r, n).start()

    def multiply(j, r, b, k, half, strip):
        dst = xs if j == 0 else us
        base = column(j, r)
        pz, py = place(r, k, b)
        chip = pz * 4 + py
        at = pl.multiple_of(32 * chip, 32)
        w = 512 if j == 0 else 256
        pm = pmat[chip]
        for off in range(0, JOBS[j], w):
            got = dot(pm, stage[half, r, k, :, :, pl.ds(strip + off, w)].reshape(256, w))
            cols = pl.ds(base + off, w)
            dst[0, pl.ds(at, 32), cols] = got[0:32].astype(BF)
            dst[1, pl.ds(at, 32), cols] = got[32:64].astype(BF)
            ov[pl.ds(pl.multiple_of(8 * chip, 8), 8), cols] = got[64:72]

    def dispatch_tokens(n):
        for r in range(2):
            load(0, r, n).wait()

            def body(k, c, r=r):
                multiply(0, r, order(r, n), k, n % 2, 0)
                return c

            lax.fori_loop(0, 4, body, 0)
        if n == 3:
            overflow(0, 0)
            overflow(0, 1)

    def dispatch_upstream(j):
        for r in range(2):
            for n in range(4):
                load(j, r, n).wait()

                def body(k, c, r=r, n=n):
                    multiply(j, r, order(r, n), k, (j - 1) % 2, 256 * n)
                    return c

                lax.fori_loop(0, 4, body, 0)
            overflow(j, r)

    def overflow(j, r):
        dst = xs if j == 0 else us
        row, col = iota((64, 128), 0), iota((64, 128), 1)
        w = 512 if j == 0 else 256
        for e in range(2):
            sel = jnp.where(col == 8 * (row // 4) + 4 * e + row % 4, 1.0, 0.0).astype(BF)
            for off in range(0, JOBS[j], w):
                cols = pl.ds(column(j, r) + off, w)
                dst[e, 512:576, cols] = dot(sel, ov[:, cols].astype(BF)).astype(BF)

    def share_routing():
        def body(i, c):
            p = lax.rem(me + i, NE)
            pltpu.make_async_remote_copy(
                src_ref=meta,
                dst_ref=metas.at[me],
                send_sem=mt_s,
                recv_sem=mt_r,
                device_id=(x, p),
                device_id_type=MESH,
            ).start()
            return c

        lax.fori_loop(1, NE, body, 0)

    def read_routing():
        metas[me] = meta[...]
        part = metas.at[pl.ds(0, NE - 1)]
        pltpu.make_async_copy(part, part, mt_s).wait()
        pltpu.make_async_copy(part, part, mt_r).wait()
        known = metas[...].astype(F32)
        before = jnp.where(iota((128, 128), 0) < iota((128, 128), 1), 1.0, 0.0).astype(BF)
        for e in range(2):
            hit = jnp.where(known[:, 0:8, :] == (2 * me + e).astype(F32), 1.0, 0.0)
            routed = jnp.sum(hit, axis=1)
            gates = jnp.sum(hit * known[:, 8:16, :], axis=1)
            number = jnp.where(routed > 0, dot(routed.astype(BF), before) + 1.0, 0.0)
            for h in range(2):
                pick = jnp.where(iota((16, NE), 1) == 2 * iota((16, NE), 0) + h, 1.0, 0.0).astype(BF)
                ranks[e, :, 128 * h : 128 * h + 128] = dot(pick, number.astype(BF))
                ranks[2 + e, :, 128 * h : 128 * h + 128] = dot(pick, gates.astype(BF))

    def build_dispatch():
        def body(chip, c):
            at = pl.multiple_of(32 * chip, 32)

            def rows(n):
                pair = [jnp.broadcast_to(ranks[n + e, pl.ds(chip, 1), :], (80, 256)) for e in range(2)]
                return jnp.where(second > 0.5, pair[1], pair[0])

            pm = jnp.where(rows(0) == target, 1.0, 0.0)
            pmat[chip] = pm.astype(BF)
            got = jnp.broadcast_to(jnp.sum(pm * rows(2), axis=1, keepdims=True), (80, 128))
            xgate[0, pl.ds(at, 32), :] = got[0:32]
            xgate[1, pl.ds(at, 32), :] = got[32:64]
            ov[pl.ds(pl.multiple_of(8 * chip, 8), 8), D : D + 128] = got[64:72]
            return c

        lax.fori_loop(0, 16, body, 0)
        row, col = iota((64, 128), 0), iota((64, 128), 1)
        for e in range(2):
            sel = jnp.where(col == 8 * (row // 4) + 4 * e + row % 4, 1.0, 0.0).astype(BF)
            xgate[e, 512:576, :] = dot(sel, ov[:, D : D + 128].astype(BF))

    def gate_of(e, rows):
        return xgate[e, rows, 0:1]

    def forward(e, lo, hi):
        if lo == 0:
            for cp in wload(e):
                cp.wait()

        def body(i, c):
            rows = pl.ds(pl.multiple_of((i // 3) * 192, 192), 192)
            cols = pl.ds(pl.multiple_of((i % 3) * 256, 256), 256)
            pg = dot(xs[e, rows, :], wgv[:, cols])
            pu = dot(xs[e, rows, :], wuv[:, cols])
            pre_g[e, rows, cols] = pg
            pre_u[e, rows, cols] = pu
            hidden = pg * jax.nn.sigmoid(pg) * pu
            wh[e, rows, cols] = (gate_of(e, rows) * hidden).astype(BF)
            return c

        lax.fori_loop(lo, hi, body, 0)

    def backward(e):
        wdload(e).wait()

        def body(i, c):
            rows = pl.ds(pl.multiple_of((i // 3) * 192, 192), 192)
            cols = pl.ds(pl.multiple_of((i % 3) * 256, 256), 256)
            raw = dot_nt(us[e, rows, :], wdv[cols, :])
            pg, pu = pre_g[e, rows, cols], pre_u[e, rows, cols]
            s = jax.nn.sigmoid(pg)
            act = pg * s
            part = raw * (act * pu)
            part = part[:, 0:128] + part[:, 128:256]
            dgacc[rows, :] = jnp.where(i % 3 == 0, jnp.zeros_like(part), dgacc[rows, :]) + part
            dh = gate_of(e, rows) * raw
            dgu[e, 0, rows, cols] = (dh * pu * s * (1.0 + pg * (1.0 - s))).astype(BF)
            dgu[e, 1, rows, cols] = (dh * act).astype(BF)
            return c

        lax.fori_loop(0, 9, body, 0)
        if e == 0:
            wdload(1).start()

    def input_grad(e):
        for cp in wload(e):
            cp.wait()

        def body(i, c):
            rows = pl.ds(pl.multiple_of((i // 4) * 192, 192), 192)
            cols = pl.ds(pl.multiple_of((i % 4) * 512, 512), 512)
            dx = dot_nt(dgu[e, 0, rows, :], wgv[cols, :]) + dot_nt(dgu[e, 1, rows, :], wuv[cols, :])
            dxs[e, rows, cols] = dx.astype(BF)
            return c

        lax.fori_loop(0, 12, body, 0)
        r, col = iota((512, 64), 0), iota((512, 64), 1)
        place = 2 * (r // 16) + (r % 16) // 8 == col
        packed = jnp.zeros((512, 256), F32)
        for q in range(8):
            sel = jnp.where(place & (r % 8 == q), 1.0, 0.0).astype(BF)
            packed = packed + dot(sel, dxs[e, 512:576, 256 * q : 256 * q + 256])
        dxs[e, 0:512, D : D + 256] = packed.astype(BF)
        dgate = jnp.sum(dgacc[...], axis=1, keepdims=True).astype(BF).astype(F32)
        first = iota((512, 128), 1) == 0
        sel = jnp.where(place & (r % 8 == 0), 1.0, 0.0).astype(BF)
        over = dot(sel, jnp.broadcast_to(dgate[512:576], (64, 128)).astype(BF))
        main = jnp.broadcast_to(dgate[0:512], (512, 128))
        dxs[e, 0:512, D + 256 :] = jnp.where(first, main, over).astype(BF)

    def send_back(e):
        pltpu.make_async_copy(dxs.at[e, pl.ds(pl.multiple_of(16 * me, 16), 16)], back.at[e, pl.ds(pl.multiple_of(16 * me, 16), 16)], ld_sem.at[2]).start()

        def body(i, c):
            p = lax.rem(me + i, NE)
            pltpu.make_async_remote_copy(
                src_ref=dxs.at[e, pl.ds(pl.multiple_of(16 * p, 16), 16)],
                dst_ref=back.at[e, pl.ds(pl.multiple_of(16 * me, 16), 16)],
                send_sem=bk_s.at[e],
                recv_sem=bk_r.at[e],
                device_id=(x, p),
                device_id_type=MESH,
            ).start()
            return c

        lax.fori_loop(1, NE, body, 0)
        pltpu.make_async_copy(dxs.at[e, pl.ds(pl.multiple_of(16 * me, 16), 16)], back.at[e, pl.ds(pl.multiple_of(16 * me, 16), 16)], ld_sem.at[2]).wait()

    def wait_back(e):
        part = back.at[e, pl.ds(0, 16 * (NE - 1))]
        pltpu.make_async_copy(part, part, bk_s.at[e]).wait()
        pltpu.make_async_copy(part, part, bk_r.at[e]).wait()

    chunks = [("d", 0), ("d", 1), ("g", 0), ("u", 0), ("g", 1), ("u", 1)]

    def partial(m, quarter, half):
        kind, e = chunks[m]
        cols = pl.ds(pl.multiple_of(quarter * 512 + half * 256, 256), 256)
        a = (us if kind == "d" else xs)[e, :, cols]
        b = wh[e] if kind == "d" else dgu[e, 0 if kind == "g" else 1]
        return dot_tn(a, b)

    def sa_copy(m, d):
        return pltpu.make_async_remote_copy(
            src_ref=sa.at[m % 2, pl.ds(256 * d, 256)],
            dst_ref=ra.at[m, d],
            send_sem=sa_s.at[m, d],
            recv_sem=ra_r.at[m, d],
            device_id=((right, left)[d], me),
            device_id_type=MESH,
        )

    def sb_copy(m, d, h):
        rows = pl.ds(256 * h, 256)
        return pltpu.make_async_remote_copy(
            src_ref=sb.at[m % 2, d, rows],
            dst_ref=rb.at[m, d, rows],
            send_sem=sb_s.at[m, d, h],
            recv_sem=rb_r.at[m, d, h],
            device_id=((right, left)[d], me),
            device_id_type=MESH,
        )

    def step_a(m):
        for d in range(2):
            if m >= 2:
                sa_copy(m - 2, d).wait_send()
            sa[m % 2, 256 * d : 256 * d + 256, :] = partial(m, lax.rem(x + 2, NX), d).astype(BF)
            sa_copy(m, d).start()

    def step_b(m, h):
        for d in range(2):
            if m >= 2:
                sb_copy(m - 2, d, h).wait_send()
            total = partial(m, (right, left)[d], h)
            if h == d:
                sa_copy(m, d).wait_recv()
                total = total + ra[m, d].astype(F32)
            sb[m % 2, d, 256 * h : 256 * h + 256, :] = total.astype(BF)
            sb_copy(m, d, h).start()

    outs = {"d": gd, "g": gg, "u": gu}

    def out_copy(m):
        kind, e = chunks[m]
        return pltpu.make_async_copy(outd if kind == "d" else outv.at[m % 2], outs[kind].at[e], out_sem.at[m])

    def own_part(m):
        for h in range(2):
            own[256 * h : 256 * h + 256, :] = partial(m, x, h)

    def final(m):
        kind, e = chunks[m]
        own_part(m)
        if m == 1:
            out_copy(0).wait()
        if m >= 4:
            out_copy(m - 2).wait()
        for d in range(2):
            for h in range(2):
                sb_copy(m, d, h).wait_recv()
            pltpu.make_async_copy(rb.at[m, d], rbv.at[d], ld_sem.at[d]).start()
        for d in range(2):
            pltpu.make_async_copy(rb.at[m, d], rbv.at[d], ld_sem.at[d]).wait()

        def body(i, c):
            rows = pl.ds(pl.multiple_of(i * 128, 128), 128)
            total = own[rows, :] + rbv[0, rows, :].astype(F32) + rbv[1, rows, :].astype(F32)
            if kind == "d":
                outd[:, rows] = total.T.astype(BF)
            else:
                outv[m % 2, rows, :] = total.astype(BF)
            return c

        lax.fori_loop(0, 4, body, 0)
        out_copy(m).start()

    def combine():
        id_rows = ids[...].astype(F32).T.astype(jnp.int32)
        rank = slot_numbers(id_rows)
        dvals = jnp.zeros((128, 64), F32)
        for half in range(2):
            wait_back(half)
            loads = []
            for q in range(4):
                rows = pl.ds(128 * q, 128)
                for n, (at, w) in enumerate(((0, 1024), (1024, 1024), (D, 384))):
                    dst = stage.at[n // 2, n % 2, q // 2, q % 2, :, pl.ds(0, w)]
                    loads.append(pltpu.make_async_copy(back.at[half, rows, pl.ds(at, w)], dst, bk_l.at[q, n]))
            for load in loads:
                load.start()

            def held(n, at, w):
                return stage[n // 2, n % 2, 0:2, :, :, at : at + w].reshape(512, w)

            spread = jnp.where(iota((64, 512), 0) == 2 * (iota((64, 512), 1) // 16) + half, 1.0, 0.0).astype(BF)
            wide = dot(rank, spread)
            lane = iota((128, 512), 1) % 16
            pm = jnp.where(wide == (lane + 1).astype(F32), 1.0, 0.0).astype(BF)
            for load in loads:
                load.wait()
            for n in range(4):
                cols = slice(512 * n, 512 * n + 512)
                got = dot(pm, held(n // 2, 512 * (n % 2), 512))
                tokacc[:, cols] = got if half == 0 else tokacc[:, cols] + got
            over = held(2, 0, 256)
            info = held(2, 256, 128).astype(F32)
            own_expert = iota((512, 64), 1) == 2 * (iota((512, 64), 0) // 16) + half
            for q in range(8):
                po = jnp.where((wide == (17 + lane // 8).astype(F32)) & (lane % 8 == q), 1.0, 0.0).astype(BF)
                cols = slice(256 * q, 256 * q + 256)
                tokacc[:, cols] = tokacc[:, cols] + dot(po, over)
                if q == 0:
                    dvals = dvals + dot(po, jnp.where(own_expert, info[:, 1:2], 0.0).astype(BF))
            dvals = dvals + dot(pm, jnp.where(own_expert, info[:, 0:1], 0.0).astype(BF))
        gtok[...] = tokacc[...].astype(BF)
        expert = iota((128, 64), 1)
        picked = [
            jnp.sum(jnp.where(id_rows[:, k : k + 1] == expert, dvals, 0.0), axis=1, keepdims=True) for k in range(8)
        ]
        dgate = jnp.concatenate(picked, axis=1)
        dgate = dgate.T
        glog[...] = probs * (dgate - jnp.sum(probs * dgate, axis=0, keepdims=True))

    own_rows = [
        pltpu.make_async_copy(src, dxs.at[i, pl.ds(0, 128), pl.ds(0, D)], ld_sem.at[i])
        for i, src in enumerate((tokens, upstream))
    ]
    for cp in own_rows:
        cp.start()
    raised = jnp.exp(logits[...] - jnp.max(logits[...], axis=0, keepdims=True))
    probs = raised / jnp.sum(raised, axis=0, keepdims=True)
    meta[...] = jnp.concatenate([ids[...].astype(F32), probs.astype(BF).astype(F32)], axis=0).astype(BF)
    for cp in own_rows:
        cp.wait()
    pl.semaphore_wait(barrier, NE - 1 + 2)

    ag_own(0)
    share_routing()
    ag_ring(0)
    ag_chunk(0)
    ag_own(1)
    start_weights(0)
    wdload(0).start()
    read_routing()
    build_dispatch()
    fetch(0, 0)
    dispatch_tokens(0)
    ag_forward(0)
    fetch(0, 1)
    fetch(0, 2)
    ag_ring(1)
    dispatch_tokens(1)
    ag_chunk(1)
    dispatch_tokens(2)
    ag_own(2)
    ag_last(0)
    fetch(1, 0)
    fetch(0, 3)
    ag_forward(1)
    dispatch_tokens(3)
    fetch(1, 1)
    fetch(1, 2)
    ag_ring(2)
    forward(0, 0, 5)
    ag_chunk(2)
    ag_last(1)
    forward(0, 5, 9)
    fetch(1, 3)
    start_weights(1)
    dispatch_upstream(1)
    step_a(0)
    ag_own(3)
    ag_forward(2)
    forward(1, 0, 5)
    ag_ring(3)
    ag_last(2)
    forward(1, 5, 9)
    start_weights(0)
    step_a(1)
    ag_chunk(3)
    for n in range(4):
        fetch(2, n)
    dispatch_upstream(2)
    step_b(0, 0)
    ag_own(4)
    ag_forward(3)
    step_b(1, 0)
    ag_last(3)
    ag_ring(4)
    ag_chunk(4)
    for n in range(4):
        fetch(3, n)
    dispatch_upstream(3)
    step_b(0, 1)
    step_b(1, 1)
    ag_forward(4)
    ag_last(4)
    for n in range(4):
        fetch(4, n)
    dispatch_upstream(4)
    backward(0)
    step_a(2)
    for j in range(NJ):
        for r in range(2):
            for k in range(2):
                ag(j, r, k).wait_send()
    input_grad(0)
    start_weights(1)
    send_back(0)
    backward(1)
    step_b(2, 0)
    step_b(2, 1)
    step_a(3)
    input_grad(1)
    send_back(1)
    final(0)
    final(1)
    step_b(3, 0)
    step_b(3, 1)
    step_a(4)
    final(2)
    step_b(4, 0)
    step_b(4, 1)
    step_a(5)
    final(3)
    step_b(5, 0)
    step_b(5, 1)
    final(4)
    combine()
    final(5)
    for m in (4, 5):
        for d in range(2):
            sa_copy(m, d).wait_send()
            for h in range(2):
                sb_copy(m, d, h).wait_send()
    for m in (1, 4, 5):
        out_copy(m).wait()
    for j in range(NJ):
        for r in range(2):
            for k in range(2, 12):
                ag(j, r, k).wait_send()


def hand_over(*refs):
    src, dst, mid, sems = refs[0:5], refs[5:10], refs[10:15], refs[15]
    loads = [pltpu.make_async_copy(src[i], mid[i], sems.at[0, i]) for i in range(5)]
    stores = [pltpu.make_async_copy(mid[i], dst[i], sems.at[1, i]) for i in range(5)]
    for load in loads:
        load.start()
    for load, store in zip(loads, stores):
        load.wait()
        store.start()
    for store in stores:
        store.wait()


def on_device(tokens, expert_ids, gate_logits, upstream, w_gate, w_up, w_down):
    sd = jax.ShapeDtypeStruct
    dma = pltpu.SemaphoreType.DMA
    vm = pltpu.VMEM
    res = pl.pallas_call(
        kernel,
        out_shape=(
            sd((128, D), BF),
            sd((8, 128), F32),
            sd((2, 512, FF), BF),
            sd((2, 512, FF), BF),
            sd((2, FF, 512), BF),
            sd((6, 2, 512, FF), BF),
            sd((2, NE * 16, BACK), BF),
            *[sd((4, 4, 2, 128, w), BF) for w in JOBS for _ in range(2)],
        ),
        in_specs=[ANY] * 5 + [VMEM] * 2,
        out_specs=(VMEM, VMEM) + (ANY,) * 15,
        scratch_shapes=[
            vm((16, 128), BF),
            vm((NE, 16, 128), BF),
            vm((4, 16, 256), F32),
            vm((2, 2, 4, 2, 128, 1024), BF),
            vm((16, 80, 256), BF),
            vm((2, ROWS, D), BF),
            vm((2, ROWS, D), BF),
            vm((128, D + 128), F32),
            vm((2, ROWS, 128), F32),
            vm((D, FF), BF),
            vm((D, FF), BF),
            vm((FF, D), BF),
            vm((2, ROWS, FF), F32),
            vm((2, ROWS, FF), F32),
            vm((2, ROWS, FF), BF),
            vm((2, 2, ROWS, FF), BF),
            vm((ROWS, 128), F32),
            vm((2, 512, FF), BF),
            vm((6, 2, 256, FF), BF),
            vm((2, 2, 512, FF), BF),
            vm((2, 512, FF), BF),
            vm((512, FF), F32),
            vm((2, 512, FF), BF),
            vm((FF, 512), BF),
            vm((2, ROWS, BACK), BF),
            vm((128, D), F32),
            dma,
            dma,
            dma((NJ, 2, 12)),
            dma((NJ, 2, 12)),
            dma((NJ, 2)),
            dma((2, 2, 4)),
            dma((3,)),
            dma((6, 2)),
            dma((6, 2)),
            dma((6, 2, 2)),
            dma((6, 2, 2)),
            dma((2,)),
            dma((2,)),
            dma((4, 3)),
            dma((4,)),
            dma((6,)),
        ],
        compiler_params=pltpu.CompilerParams(collective_id=0, has_side_effects=True, vmem_limit_bytes=64 << 20),
        cost_estimate=pl.CostEstimate(flops=29 * 10**9, bytes_accessed=10**8, transcendentals=10**6),
        name="expert_backward",
    )(tokens, upstream, w_gate, w_up, w_down, expert_ids.T, gate_logits.T)
    done = pl.pallas_call(
        hand_over,
        out_shape=tuple(sd(r.shape, r.dtype) for r in res[:5]),
        in_specs=[ANY] * 5,
        out_specs=(ANY,) * 5,
        scratch_shapes=[vm(r.shape, r.dtype) for r in res[:5]] + [dma((2, 5))],
        name="hand_over",
    )(*res[:5])
    return (done[0], done[1].T) + tuple(done[2:])


def solution(mesh):
    rows = P(("dp", "expert"), None)
    whole = P("expert", None, None)
    return jax.shard_map(
        on_device,
        mesh=mesh,
        in_specs=(rows, rows, rows, rows, whole, whole, whole),
        out_specs=(rows, rows, P("expert", "dp", None), P("expert", "dp", None), P("expert", None, "dp")),
        check_vma=False,
    )
```

time: 290 us -> 269 us (0.928)
  local copies, waits for them, and re-layouts: 12.1 us -> 0 us
  Pallas kernels: 276 us -> 267 us
    unnamed x11 -> x0, local copies, waits for them, and re-layouts: 12.1 us -> none
    pallas_call x1 -> x2, Pallas kernels: 276 us -> 267 us  [the longest x1 263 us: on_device(): pl.pallas_call(kernel, out_shape=(sd((128, D), BF), sd((8, 128), F32), sd...]
where the time goes in v3:
time: 269 us; the launch traced here: 268 us
  Pallas kernels  267 us (99%)
    pallas_call x1, Pallas kernels, on_device(): pl.pallas_call(kernel, out_shape=(sd((128, D), BF), sd((8, 128), F32), sd...  263 us

profile of v3, /device:TPU:1, one launch (start us, length us, event | category | flops | bytes accessed | tf_op | source)
XLA Modules:
  0.0 268.2 jit_solution(18403190313734335311)
XLA Ops:
  0.6 263.0 %expert_backward.1 = (bf16[128,2048]{1,0:T(8,128)(2,1)}, f32[8,128]{1,0:T(8,128)}, bf16[2,512,768]{2,1,0:T(8,128)(2,1)}, bf16[2,512,768]{2,1,0:T(8,128)(2,1)}, b...) custom-call(bf16[128,2048]{1,0:T(8,128)(2,1)} %tokens.1, ...), custom_call_target="tpu_custom_call" | custom-call | flops 28999999488 | bytes 100000000 | tf_op jit(solution)/shard_map/expert_backward/pallas_call | solution.py:668
  263.6 4.4 %hand_over.1 = (bf16[128,2048]{1,0:T(8,128)(2,1)}, f32[8,128]{1,0:T(8,128)}, bf16[2,512,768]{2,1,0:T(8,128)(2,1)}, bf16[2,512,768]{2,1,0:T(8,128)(2,1)}, bf16[2,768,512]{2,1,0:T(8,128)(2,1)}) custom-call(bf16[128,2048]{1,0:T(8,128)(2,1)} %get-tuple-element.15.refs_0_, f32[8,128]{1,0:T(8,128)} %get-tuple-element.16.refs_1_, ...), custom_call_target="tpu_custom_call" | custom-call | tf_op jit(solution)/shard_map/hand_over/pallas_call | solution.py:730

commit v4 on v3

--- a/solution.py
+++ b/solution.py
@@ -585,28 +585,29 @@
     start_weights(0)
     step_a(1)
     ag_chunk(3)
+    ag_own(4)
     for n in range(4):
         fetch(2, n)
     dispatch_upstream(2)
+    ag_ring(4)
+    ag_forward(3)
     step_b(0, 0)
-    ag_own(4)
-    ag_forward(3)
+    ag_chunk(4)
+    ag_last(3)
     step_b(1, 0)
-    ag_last(3)
-    ag_ring(4)
-    ag_chunk(4)
     for n in range(4):
         fetch(3, n)
     dispatch_upstream(3)
+    ag_forward(4)
     step_b(0, 1)
+    ag_last(4)
     step_b(1, 1)
-    ag_forward(4)
-    ag_last(4)
     for n in range(4):
         fetch(4, n)
     dispatch_upstream(4)
     backward(0)
     step_a(2)
+    step_a(3)
     for j in range(NJ):
         for r in range(2):
             for k in range(2):
@@ -614,21 +615,20 @@
     input_grad(0)
     start_weights(1)
     send_back(0)
-    backward(1)
     step_b(2, 0)
     step_b(2, 1)
-    step_a(3)
+    backward(1)
     input_grad(1)
     send_back(1)
-    final(0)
-    final(1)
     step_b(3, 0)
     step_b(3, 1)
     step_a(4)
+    step_a(5)
+    final(0)
+    final(1)
     final(2)
     step_b(4, 0)
     step_b(4, 1)
-    step_a(5)
     final(3)
     step_b(5, 0)
     step_b(5, 1)

time: 269 us -> 252 us (0.937)
  Pallas kernels: 267 us -> 251 us
    pallas_call x1, Pallas kernels: 263 us -> 247 us  [on_device(): pl.pallas_call(kernel, out_shape=(sd((128, D), BF), sd((8, 128), F32), sd...]
where the time goes in v4:
time: 252 us
  Pallas kernels  251 us (100%)
    pallas_call x1, Pallas kernels, on_device(): pl.pallas_call(kernel, out_shape=(sd((128, D), BF), sd((8, 128), F32), sd...  247 us

profile of v4, /device:TPU:1, one launch (start us, length us, event | category | flops | bytes accessed | tf_op | source)
XLA Modules:
  0.0 251.9 jit_solution(4232801459192800741)
XLA Ops:
  0.6 246.7 %expert_backward.1 = (bf16[128,2048]{1,0:T(8,128)(2,1)}, f32[8,128]{1,0:T(8,128)}, bf16[2,512,768]{2,1,0:T(8,128)(2,1)}, bf16[2,512,768]{2,1,0:T(8,128)(2,1)}, b...) custom-call(bf16[128,2048]{1,0:T(8,128)(2,1)} %tokens.1, ...), custom_call_target="tpu_custom_call" | custom-call | flops 28999999488 | bytes 100000000 | tf_op jit(solution)/shard_map/expert_backward/pallas_call | solution.py:668
  247.4 4.4 %hand_over.1 = (bf16[128,2048]{1,0:T(8,128)(2,1)}, f32[8,128]{1,0:T(8,128)}, bf16[2,512,768]{2,1,0:T(8,128)(2,1)}, bf16[2,512,768]{2,1,0:T(8,128)(2,1)}, bf16[2,768,512]{2,1,0:T(8,128)(2,1)}) custom-call(bf16[128,2048]{1,0:T(8,128)(2,1)} %get-tuple-element.15.refs_0_, f32[8,128]{1,0:T(8,128)} %get-tuple-element.16.refs_1_, ...), custom_call_target="tpu_custom_call" | custom-call | tf_op jit(solution)/shard_map/hand_over/pallas_call | solution.py:730
